TPU v7x, 32 devices: a whole 2x2x4 slice. The times are simulated.
32 devices in a mesh: ang: 16 (over z, y, core), dist: 2 (over x).
Axes of the slice: x: 2, y: 2, z: 4, core: 2. Of those that a mesh axis runs over, the one named last changes fastest.
Arguments:
- volume: float32 [16, 1024, 1024], P('ang', 'dist'), may hold values from -0.2 to 0.2
- row_weights: float32 [64, 1024], replicated, may hold values from 0.2 to 2
- angle_slope: int32 [64], replicated, may hold values from -1024 to 1023, as said below
- shear_index: int32 [64, 1024], replicated, may hold values from 0 to 1022, as said below
- shear_weight: float32 [64, 1024], replicated, as said below
- fresnel: float32 [2], P('dist'), may hold values from 20 to 80
- measured: float32 [2, 64, 16, 1024], P('dist', 'ang'), may hold values from 0.3 to 1.7
Outputs:
- volume_grad: float32 [16, 1024, 1024], P('ang', 'dist')
Inputs may be any that keep to these rules, and one draw needn't show every extreme that they name: `angle_slope`: distinct values, one in each of 64 equal runs of the range, in an order drawn from the seed. shear_index[a, u] = floor(P[a, u] / 4096) + 512 with P[a, u] = (3072 + angle_slope[a]) * (u - 512). shear_weight[a, u] = (P[a, u] mod 4096) / 4096 with the same P.
All inputs are finite; a program needn't handle non-finite values.
Results may differ from a plain program's by a relative error of at most 0.0003.
Values sent between devices are 32-bit elements; how exact they have to be, the bound alone decides.
A program may use at most 64 MiB of HBM per device.

v0:
```python
from functools import partial
import math

import jax
import jax.numpy as jnp
from jax import lax
from jax.sharding import PartitionSpec as P

ABSORB = 0.1
HIGHEST = lax.Precision.HIGHEST


def signed_freq(counter, length):
    signed = jnp.where(counter <= (length - 1) // 2, counter, counter - length)
    return signed.astype(jnp.float32) / length


def dft_table(length):
    counter = jnp.arange(length, dtype=jnp.int32)
    twiddle_angle = (counter[:, None] * counter[None, :] % length).astype(jnp.float32) * (
        2.0 * math.pi / length
    )
    return (jnp.cos(twiddle_angle), jnp.sin(twiddle_angle))


def build_tables(slice_count, grid_width):
    inner_len = math.gcd(grid_width, 128)
    outer_len = grid_width // inner_len
    z_cos, z_sin = dft_table(slice_count)
    q_cos, q_sin = dft_table(outer_len)
    p_cos, p_sin = dft_table(inner_len)
    outer_count = jnp.arange(outer_len, dtype=jnp.int32)
    inner_count = jnp.arange(inner_len, dtype=jnp.int32)
    mixed = (outer_count[:, None] * inner_count[None, :] % grid_width).astype(jnp.float32) * (
        2.0 * math.pi / grid_width
    )
    return (z_cos, z_sin, q_cos, q_sin, p_cos, p_sin, jnp.cos(mixed), jnp.sin(mixed))


def table_product(real_part, imag_part, cos_table, sin_table, sign_value, joined):
    real_row = jnp.stack([cos_table, sign_value * sin_table], axis=1)
    imag_row = jnp.stack([-sign_value * sin_table, cos_table], axis=1)
    block_table = jnp.stack([real_row, imag_row], axis=0)
    stacked = jnp.stack([real_part, imag_part], axis=0)
    result = jnp.einsum(joined, stacked, block_table, precision=HIGHEST)
    return (result[0], result[1])


def twiddle(real_part, imag_part, cos_table, sin_table, sign_value):
    return (
        real_part * cos_table - sign_value * imag_part * sin_table,
        imag_part * cos_table + sign_value * real_part * sin_table,
    )


def forward_transform(real_part, imag_part, tables):
    z_cos, z_sin, q_cos, q_sin, p_cos, p_sin, mix_cos, mix_sin = tables
    angle_count, slice_count, grid_width = real_part.shape
    shape_four = (angle_count, slice_count, q_cos.shape[0], p_cos.shape[0])
    real_part = real_part.reshape(shape_four)
    imag_part = imag_part.reshape(shape_four)
    real_part, imag_part = table_product(
        real_part, imag_part, q_cos, q_sin, -1.0, "cazqp,cqdk->dazkp"
    )
    real_part, imag_part = twiddle(real_part, imag_part, mix_cos, mix_sin, -1.0)
    real_part, imag_part = table_product(
        real_part, imag_part, p_cos, p_sin, -1.0, "cazkp,cpdm->dazkm"
    )
    return table_product(real_part, imag_part, z_cos, z_sin, -1.0, "cazkm,czdy->daykm")


def inverse_transform(real_part, imag_part, tables):
    z_cos, z_sin, q_cos, q_sin, p_cos, p_sin, mix_cos, mix_sin = tables
    angle_count = real_part.shape[0]
    slice_count = real_part.shape[1]
    real_part, imag_part = table_product(
        real_part, imag_part, z_cos, z_sin, 1.0, "caykm,cydz->dazkm"
    )
    real_part, imag_part = table_product(
        real_part, imag_part, p_cos, p_sin, 1.0, "cazkm,cmdp->dazkp"
    )
    real_part, imag_part = twiddle(real_part, imag_part, mix_cos, mix_sin, 1.0)
    real_part, imag_part = table_product(
        real_part, imag_part, q_cos, q_sin, 1.0, "cazkp,ckdq->dazqp"
    )
    grid_width = q_cos.shape[0] * p_cos.shape[0]
    return (
        real_part.reshape(angle_count, slice_count, grid_width),
        imag_part.reshape(angle_count, slice_count, grid_width),
    )


def image_loss(images, measured_set, fresnel_set, angles_total):
    slice_count = images.shape[1]
    grid_width = images.shape[2]
    tables = build_tables(slice_count, grid_width)
    outer_len = tables[2].shape[0]
    inner_len = tables[4].shape[0]
    attenuation = jnp.exp(-ABSORB * images)
    spec_real, spec_imag = forward_transform(
        attenuation * jnp.cos(images), attenuation * jnp.sin(images), tables
    )
    freq_rows = signed_freq(jnp.arange(slice_count, dtype=jnp.int32), slice_count)
    column_order = (
        outer_len * jnp.arange(inner_len, dtype=jnp.int32)[None, :]
        + jnp.arange(outer_len, dtype=jnp.int32)[:, None]
    )
    freq_cols = signed_freq(column_order, grid_width)
    square_sum = freq_rows[:, None, None] ** 2 + freq_cols[None, :, :] ** 2
    norm_factor = 1.0 / (slice_count * grid_width)
    phase_table = math.pi * fresnel_set[0] * square_sum
    phase_cos = jnp.cos(phase_table)
    phase_sin = jnp.sin(phase_table)
    prop_real = spec_real * phase_cos + spec_imag * phase_sin
    prop_imag = spec_imag * phase_cos - spec_real * phase_sin
    field_real, field_imag = inverse_transform(prop_real, prop_imag, tables)
    intensity = (field_real * norm_factor) ** 2 + (field_imag * norm_factor) ** 2
    total = jnp.sum((intensity - measured_set[0]) ** 2)
    return total / angles_total


def resample(rays, shear_index, shear_weight, path_scale):
    lower_index = shear_index[:, None, :]
    lower_tap = jnp.take_along_axis(rays, lower_index, axis=2)
    upper_tap = jnp.take_along_axis(rays, lower_index + 1, axis=2)
    weight_col = shear_weight[:, None, :]
    return path_scale[:, None, None] * ((1.0 - weight_col) * lower_tap + weight_col * upper_tap)


def spread_back(gradient, shear_index, shear_weight, path_scale):
    zero_rays = jnp.zeros(gradient.shape, jnp.float32)
    linear_map = partial(
        resample, shear_index=shear_index, shear_weight=shear_weight, path_scale=path_scale
    )
    return jax.vjp(linear_map, zero_rays)[1](gradient)[0]


def shards(volume, row_weights, angle_slope, shear_index, shear_weight, fresnel, measured):
    row_count = volume.shape[1]
    angles_total = row_weights.shape[0]
    dist_index = lax.axis_index("dist")
    row_start = dist_index * row_count
    path_scale = jnp.sqrt(1.0 + (angle_slope.astype(jnp.float32) / 512.0) ** 2)
    own_weights = lax.dynamic_slice_in_dim(row_weights, row_start, row_count, 1)
    rays = jnp.einsum(
        "ay,zyx->azx",
        row_weights,
        lax.all_gather(volume, "dist", axis=1, tiled=True),
        precision=HIGHEST,
    )
    projections = resample(rays, shear_index, shear_weight, path_scale)
    images = lax.all_to_all(projections, "ang", split_axis=0, concat_axis=1, tiled=True)
    local_loss = partial(
        image_loss, measured_set=measured, fresnel_set=fresnel, angles_total=angles_total
    )
    image_grads = jax.vjp(local_loss, images)[1](jnp.ones((), jnp.float32))[0]
    outgoing = lax.psum(image_grads, "dist")
    returned = lax.all_to_all(outgoing, "ang", split_axis=1, concat_axis=0, tiled=True)
    spread = spread_back(returned, shear_index, shear_weight, path_scale)
    volume_grad = jnp.einsum("ay,azx->zyx", own_weights, spread, precision=HIGHEST)
    return volume_grad


def solution(mesh):
    placed = (P("ang", "dist", None), P(), P(), P(), P(), P("dist"), P("dist", "ang", None, None))
    return jax.shard_map(
        shards, mesh=mesh, in_specs=placed, out_specs=P("ang", "dist", None), check_vma=False
    )
```

profile of v0, /device:TPU:1, one launch (start us, length us, event | category | flops | bytes accessed | tf_op | source)
XLA Modules:
  0.0 2099.9 jit_solution(10414959257627189431)
XLA Ops:
  6.5 0.7 all-gather.2.cloned.1.call-update
  7.8 0.6 fusion.96
  8.6 0.7 broadcast_multiply_fusion.2
  10.2 0.6 fusion.61
  11.1 1.6 bitcast_or_fusion.1
  12.7 1.8 broadcast_add_fusion
  14.5 0.7 copy-done.6
  15.9 0.9 fusion.37
  17.2 0.7 broadcast_subtract_fusion
  17.9 49.8 %all-gather.2.cloned.1.call-done = f32[1,1024,1024]{2,1,0:T(8,128)} async-done(((f32[1,512,1024]{2,1,0:T(8,128)}), f32[1,1024,1024]{2,1,0:T(8,128)}) %all-gather.2.cloned.1.call-update) | async-done | bytes 4194320 | tf_op jit(solution)/shard_map/all_gather | solution.py:148
  67.8 4.8 fusion
  72.6 518.5 %gather_fusion = f32[65536]{0:T(1024)S(1)} fusion(f32[64,1024]{1,0:T(8,128)S(1)} %fusion, s32[65536]{0:T(1024)S(1)} %bitcast.296), kind=kCustom, calls=%fused_computation.clone | custom fusion | bytes 1048576 | tf_op jit(solution)/shard_map/jit(take_along_axis)/gather | solution.py:124
  591.2 518.5 %gather_fusion.1 = f32[65536]{0:T(1024)S(1)} fusion(f32[64,1024]{1,0:T(8,128)S(1)} %fusion, s32[65536]{0:T(1024)S(1)} %bitcast.297), kind=kCustom, calls=%fused_computation.1.clone | custom fusion | bytes 1048576 | tf_op jit(solution)/shard_map/jit(take_along_axis)/gather | solution.py:125
  1109.7 2.1 add_multiply_fusion
  1111.9 6.3 all-to-all-start
  1119.8 7.9 all-to-all-done
  1127.7 7.5 fusion.112
  1137.2 0.6 convolution_bitcast_fusion.10
  1137.9 0.6 convolution_bitcast_fusion.1
  1138.6 0.8 convolution_bitcast_fusion.9
  1139.5 0.6 convolution_bitcast_fusion.8
  1141.7 0.7 convolution_bitcast_fusion.5
  1143.5 0.9 convolution_bitcast_fusion.3
  1145.3 1.2 fusion.26
  1146.5 20.2 all-reduce.12.cloned.1.call-done
  1166.7 1.8 copy.169
  1168.5 6.7 all-to-all-start.1
  1175.8 8.8 all-to-all-done.1
  1185.0 452.2 %scatter_custom_fusion.1 = f32[65536]{0:T(1024)S(1)} fusion(s32[65536]{0:T(1024)S(1)} %bitcast.313, f32[65536]{0:T(1024)S(1)} %bitcast.315, f32[]{:T(128)} %constant.109.clone.1), kind=kCustom, calls=%fused_computation.114 | custom fusion | flops 65536 | bytes 262148
  1637.2 452.2 %scatter_custom_fusion = f32[65536]{0:T(1024)S(1)} fusion(s32[65536]{0:T(1024)S(1)} %bitcast.312, f32[65536]{0:T(1024)S(1)} %bitcast.314, f32[]{:T(128)} %constant.109.clone.1), kind=kCustom, calls=%fused_computation.116 | custom fusion | flops 65536 | bytes 262148
  2089.4 1.8 convolution_bitcast_fusion
  2091.3 1.8 copy.170
  (116 shorter events, 10.3 us)
Async XLA Ops:
  6.5 61.2 %copy-start = (f32[64,1024]{1,0:T(8,128)S(1)}, f32[64,1024]{1,0:T(8,128)}, u32[]{:S(2)}) copy-start(f32[64,1024]{1,0:T(8,128)} %param.10) | copy-start | bytes 786436
  6.5 10.2 copy-start.30
  6.5 10.7 copy-start.4
  6.5 61.2 %all-gather.2.cloned.1.call-start = ((), (), s32[]{:S(2)}) async-start(), calls=%async_computation.2 | async-start | bytes 6291456 | tf_op jit(solution)/shard_map/all_gather | solution.py:148
  591.1 518.6 %copy-start.3 = (s32[64,1024]{1,0:T(8,128)S(1)}, s32[64,1024]{1,0:T(8,128)}, u32[]{:S(2)}) copy-start(s32[64,1024]{1,0:T(8,128)} %param.12) | copy-start | bytes 786436
  591.1 518.6 %copy-start.5 = (f32[64,1024]{1,0:T(8,128)S(1)}, f32[64,1024]{1,0:T(8,128)}, u32[]{:S(2)}) copy-start(f32[64,1024]{1,0:T(8,128)} %param.13) | copy-start | bytes 786436
  591.1 518.6 %copy-start.7 = (s32[64,1024]{1,0:T(8,128)S(1)}, s32[64,1024]{1,0:T(8,128)}, u32[]{:S(2)}) copy-start(s32[64,1024]{1,0:T(8,128)} %copy-done.6) | copy-start | bytes 786436
  591.1 518.6 %copy-start.10 = (f32[64,1024]{1,0:T(8,128)S(1)}, f32[64,1024]{1,0:T(8,128)}, u32[]{:S(2)}) copy-start(f32[64,1024]{1,0:T(8,128)} %broadcast_subtract_fusion) | copy-start | bytes 786436
  591.1 518.6 %copy-start.26 = (f32[64]{0:T(128)S(1)}, f32[64]{0:T(128)}, u32[]{:S(2)}) copy-start(f32[64]{0:T(128)} %add_sqrt_fusion) | copy-start | bytes 772
  591.1 528.0 %copy-start.23 = (f32[1,8,2,8]{3,1,2,0:T(8,128)S(1)}, f32[1,8,2,8]{3,1,2,0:T(8,128)}, u32[]{:S(2)}) copy-start(f32[1,8,2,8]{3,1,2,0:T(8,128)} %get-tuple-element.46) | copy-start | bytes 1540
  591.1 528.0 %copy-start.22 = (f32[1,8,2,8]{3,1,2,0:T(8,128)S(1)}, f32[1,8,2,8]{3,1,2,0:T(8,128)}, u32[]{:S(2)}) copy-start(f32[1,8,2,8]{3,1,2,0:T(8,128)} %get-tuple-element.47) | copy-start | bytes 1540
  591.1 528.1 %copy-start.21 = (f32[1,8,2,8]{3,1,2,0:T(8,128)S(1)}, f32[1,8,2,8]{3,1,2,0:T(8,128)}, u32[]{:S(2)}) copy-start(f32[1,8,2,8]{3,1,2,0:T(8,128)} %get-tuple-element.54) | copy-start | bytes 1540
  591.2 528.2 %copy-start.20 = (f32[1,8,2,8]{3,1,2,0:T(8,128)S(1)}, f32[1,8,2,8]{3,1,2,0:T(8,128)}, u32[]{:S(2)}) copy-start(f32[1,8,2,8]{3,1,2,0:T(8,128)} %get-tuple-element.55) | copy-start | bytes 1540
  591.2 528.2 %copy-start.13 = (f32[1,4,16,1024]{3,2,1,0:T(8,128)S(1)}, f32[1,4,16,1024]{3,2,1,0:T(8,128)}, u32[]{:S(2)}) copy-start(f32[1,4,16,1024]{3,2,1,0:T(8,128)} %param.15) | copy-start | bytes 786436
  591.2 528.3 %copy-start.29 = (s32[128]{0:T(128)S(1)}, s32[128]{0:T(128)}, u32[]{:S(2)}) copy-start(s32[128]{0:T(128)} %iota_multiply_fusion) | copy-start | bytes 1540
  1109.7 26.7 %copy-start.18 = (f32[8,128]{1,0:T(8,128)S(1)}, f32[8,128]{1,0:T(8,128)}, u32[]{:S(2)}) copy-start(f32[8,128]{1,0:T(8,128)} %get-tuple-element.61) | copy-start | bytes 12292
  1109.7 26.7 %copy-start.24 = (f32[8,128]{1,0:T(8,128)S(1)}, f32[8,128]{1,0:T(8,128)}, u32[]{:S(2)}) copy-start(f32[8,128]{1,0:T(8,128)} %get-tuple-element.60) | copy-start | bytes 12292
  1109.7 26.8 %copy-start.8 = (f32[1,128,2,128]{3,1,0,2:T(8,128)S(1)}, f32[1,128,2,128]{3,1,0,2:T(8,128)}, u32[]{:S(2)}) copy-start(f32[1,128,2,128]{3,1,0,2:T(8,128)} %get-tuple-element.37) | copy-start | bytes 393220
  1109.7 26.8 %copy-start.9 = (f32[1,128,2,128]{3,1,0,2:T(8,128)S(1)}, f32[1,128,2,128]{3,1,0,2:T(8,128)}, u32[]{:S(2)}) copy-start(f32[1,128,2,128]{3,1,0,2:T(8,128)} %get-tuple-element.40) | copy-start | bytes 393220
  1111.9 25.3 %copy-start.14 = (f32[1,16,2,16]{1,3,0,2:T(8,128)S(1)}, f32[1,16,2,16]{1,3,0,2:T(8,128)}, u32[]{:S(2)}) copy-start(f32[1,16,2,16]{1,3,0,2:T(8,128)} %get-tuple-element.43) | copy-start | bytes 6148
  1111.9 25.3 %copy-start.15 = (f32[1,16,2,16]{1,3,0,2:T(8,128)S(1)}, f32[1,16,2,16]{1,3,0,2:T(8,128)}, u32[]{:S(2)}) copy-start(f32[1,16,2,16]{1,3,0,2:T(8,128)} %get-tuple-element.50) | copy-start | bytes 6148
  1111.9 15.8 all-to-all-start
  1118.2 48.5 %all-reduce.12.cloned.1.call-start = ((), (), s32[]{:S(2)}) async-start(), calls=%async_computation.3 | async-start | bytes 524288 | tf_op jit(solution)/shard_map/psum | solution.py:157
  1135.2 2.7 copy-start.16
  1135.7 2.8 copy-start.11
  1135.7 2.8 copy-start.12
  1136.4 3.0 copy-start.19
  1143.5 31.7 %copy-start.1 = (s32[64,1024,1]{1,0,2:T(8,128)S(1)}, s32[64,1024,1]{1,0,2:T(8,128)}, u32[]{:S(2)}) copy-start(s32[64,1024,1]{1,0,2:T(8,128)} %get-tuple-element.34) | copy-start | bytes 786436
  1143.5 31.7 %copy-start.2 = (s32[64,1024,1]{1,0,2:T(8,128)S(1)}, s32[64,1024,1]{1,0,2:T(8,128)}, u32[]{:S(2)}) copy-start(s32[64,1024,1]{1,0,2:T(8,128)} %get-tuple-element.35) | copy-start | bytes 786436
  1143.5 31.7 %copy-start.28 = (s32[2]{0:T(128)S(1)}, s32[2]{0:T(128)}, u32[]{:S(2)}) copy-start(s32[2]{0:T(128)} %constant.164) | copy-start | bytes 28
  1144.4 31.0 %copy-start.27 = (s32[2]{0:T(128)S(1)}, s32[2]{0:T(128)}, u32[]{:S(2)}) copy-start(s32[2]{0:T(128)} %constant.167) | copy-start | bytes 28
  1168.5 16.2 all-to-all-start.1
  (3 other events, 5.5 us)
Sparse Core Ops, SparseCore 0:
  8.9 58.8 all-gather.1
  1146.6 20.0 all-reduce.11
where the time goes:
time: 2100 us
  local copies, waits for them, and re-layouts  1040 us (50%)
  other arithmetic  927 us (44%)
  waiting for transfers between devices  87.5 us (4%)
    unnamed x6, other arithmetic  905 us
    gather x1, local copies, waits for them, and re-layouts, resample(): lower_tap = jnp.take_along_axis(rays, lower_index, axis=2)  518 us
    gather x1, local copies, waits for them, and re-layouts, resample(): upper_tap = jnp.take_along_axis(rays, lower_index + 1, axis=2)  518 us
    all_gather x1, waiting for transfers between devices, shards(): lax.all_gather(volume, 'dist', axis=1, tiled=True)  49.8 us
  transfers between devices with their start and end apart: 4, of which 4 were waited for; matrix products, arithmetic and copies ran while one was open for 1% of the time, Pallas kernels for 0%

commit v1 on v0

v1 whole, which is shorter than its diff:
```python
from functools import partial
import math

import numpy as np
import jax
import jax.numpy as jnp
from jax import lax
from jax.experimental import pallas as pl
from jax.experimental.pallas import tpu as pltpu
from jax.sharding import PartitionSpec as P

ABSORB = 0.1
HIGHEST = lax.Precision.HIGHEST
LANES = 128


def dot(a, b):
    return lax.dot_general(
        a, b, (((1,), (0,)), ((), ())), precision=HIGHEST, preferred_element_type=jnp.float32
    )


def signed_freq(counter, length):
    return np.where(counter <= (length - 1) // 2, counter, counter - length) / length


def column_tables(width):
    outer = width // LANES
    p = np.arange(LANES)
    k = np.arange(outer)
    ang = 2 * np.pi * (p[:, None] * p[None, :] % LANES) / LANES
    c, s = np.cos(ang), np.sin(ang)
    forward = np.block([[c, -s], [s, c]])
    inverse = np.block([[c, s], [-s, c]])
    mixed = 2 * np.pi * (k[:, None] * p[None, :] % width) / width
    freq2 = signed_freq(k[:, None] + outer * p[None, :], width) ** 2
    small = np.stack([np.cos(mixed), np.sin(mixed), freq2])
    return forward.astype(np.float32), inverse.astype(np.float32), small.astype(np.float32)


def row_tables(slices, angles):
    z = np.arange(slices)
    ang = 2 * np.pi * (z[:, None] * z[None, :] % slices) / slices
    trig = np.stack([np.cos(ang), np.sin(ang)])
    rows = 2 * angles * slices
    left_r = np.zeros((2, angles, slices, 2, angles, 2, slices))
    left_i = np.zeros_like(left_r)
    right = np.zeros((2, angles, 2, slices, 2, angles, slices))
    for c in range(2):
        for a in range(angles):
            for t in range(2):
                left_r[c, a, :, c, a, t, :] = trig[t]
                left_i[c, a, :, 1 - c, a, t, :] = trig[t] * (-1.0 if c == 0 else 1.0)
                right[c, a, t, :, c, a, :] = trig[t] / slices
    freq2 = np.broadcast_to(signed_freq(z, slices) ** 2, (2, angles, 2, slices)).reshape(1, -1)
    left = np.stack([left_r.reshape(rows, -1), left_i.reshape(rows, -1)])
    return left.astype(np.float32), right.reshape(-1, rows).astype(np.float32), freq2.astype(np.float32)


def fft_list(parts, sign):
    n = len(parts)
    if n == 1:
        return parts
    even = fft_list(parts[0::2], sign)
    odd = fft_list(parts[1::2], sign)
    low, high = [], []
    for k in range(n // 2):
        (er, ei), (br, bi) = even[k], odd[k]
        if k == 0:
            tr, ti = br, bi
        elif 4 * k == n:
            tr, ti = (-bi, br) if sign > 0 else (bi, -br)
        else:
            wr = math.cos(2 * math.pi * k / n)
            wi = sign * math.sin(2 * math.pi * k / n)
            tr, ti = br * wr - bi * wi, br * wi + bi * wr
        low.append((er + tr, ei + ti))
        high.append((er - tr, ei - ti))
    return low + high


def columns_forward(parts, table, mix_cos, mix_sin):
    parts = fft_list(parts, -1)
    rows = []
    for k, (re, im) in enumerate(parts):
        c, s = mix_cos[k : k + 1], mix_sin[k : k + 1]
        rows.append(jnp.concatenate([re * c + im * s, im * c - re * s], axis=1))
    return dot(jnp.concatenate(rows, axis=0), table)


def columns_inverse(spectrum, table, mix_cos, mix_sin):
    outer = mix_cos.shape[0]
    count = spectrum.shape[0] // outer
    result = dot(spectrum, table)
    parts = []
    for k in range(outer):
        re = result[k * count : (k + 1) * count, :LANES]
        im = result[k * count : (k + 1) * count, LANES:]
        c, s = mix_cos[k : k + 1], mix_sin[k : k + 1]
        parts.append((re * c - im * s, im * c + re * s))
    return fft_list(parts, 1)


def tile_pairs(outer):
    pairs = []
    half = outer // 2
    for block in range(outer):
        first = LANES * (block - half)
        ends = [first, first + LANES - 1]
        low = min(min(math.floor(u * 0.5), math.floor(u * 4095 / 4096)) for u in ends)
        high = max(max(math.floor(u * 0.5), math.floor(u * 4095 / 4096)) for u in ends) + 1
        for tile in range(low // LANES + half, high // LANES + half + 1):
            if 0 <= tile < outer:
                pairs.append((block, tile))
    return pairs


def lane_take(values, index):
    return jnp.take_along_axis(values, index, axis=1, mode="promise_in_bounds")


def band_forward(tiles, step):
    outer, count = len(tiles), tiles[0].shape[0]
    lane = lax.broadcasted_iota(jnp.int32, (1, LANES), 1).astype(jnp.float32)
    center = float(outer // 2 * LANES)
    result = [None] * outer
    for block in range(outer):
        place = step * (lane + (LANES * block - center)) * (1.0 / 4096.0)
        lower = jnp.floor(place)
        weight = place - lower
        for shift, coef in ((0.0, 1.0 - weight), (1.0, weight)):
            source = lower + (center + shift)
            tile_of = jnp.floor(source * (1.0 / LANES))
            inside = (source - LANES * tile_of).astype(jnp.int32)
            index = jnp.broadcast_to(inside, (count, LANES))
            for pair_block, tile in tile_pairs(outer):
                if pair_block != block:
                    continue
                term = jnp.where(tile_of == float(tile), coef, 0.0) * lane_take(tiles[tile], index)
                result[block] = term if result[block] is None else result[block] + term
    return result


def band_backward(blocks, step):
    outer, count = len(blocks), blocks[0].shape[0]
    lane = lax.broadcasted_iota(jnp.int32, (1, LANES), 1).astype(jnp.float32)
    center = float(outer // 2 * LANES)
    result = [None] * outer
    for tile in range(outer):
        target = (lane + (LANES * tile - center)) * 4096.0
        first = jnp.floor(target / step)
        for shift in (-1.0, 0.0, 1.0, 2.0):
            source = first + shift
            coef = jnp.maximum(4096.0 - jnp.abs(step * source - target), 0.0) * (1.0 / 4096.0)
            place = source + center
            block_of = jnp.floor(place * (1.0 / LANES))
            inside = (place - LANES * block_of).astype(jnp.int32)
            index = jnp.broadcast_to(inside, (count, LANES))
            for block, pair_tile in tile_pairs(outer):
                if pair_tile != tile:
                    continue
                term = jnp.where(block_of == float(block), coef, 0.0) * lane_take(blocks[block], index)
                result[tile] = term if result[tile] is None else result[tile] + term
    return result


def image_step(ray_tiles, slopes, fresnels, measured, tables, angles_total):
    forward, inverse, small, left, right, row_freq2 = tables
    angles, outer = len(ray_tiles), len(ray_tiles[0])
    slices = ray_tiles[0][0].shape[0]
    rows = angles * slices
    width = outer * LANES
    mix_cos, mix_sin, col_freq2 = small
    scales, steps = [], []
    for slope in slopes:
        value = slope.astype(jnp.float32)
        steps.append(value + 3072.0)
        tangent = jnp.full((1, LANES), value) * (1.0 / 512.0)
        scales.append(jnp.sqrt(1.0 + tangent * tangent))
    images = [band_forward(ray_tiles[a], steps[a]) for a in range(angles)]
    waves = []
    for q in range(outer):
        image = jnp.concatenate([images[a][q] * scales[a] for a in range(angles)], axis=0)
        fade = jnp.exp(-ABSORB * image)
        waves.append((fade * jnp.cos(image), fade * jnp.sin(image)))
    spectrum = columns_forward(waves, forward, mix_cos, mix_sin)
    spec_re = [spectrum[k * rows : (k + 1) * rows, :LANES] for k in range(outer)]
    spec_im = [spectrum[k * rows : (k + 1) * rows, LANES:] for k in range(outer)]
    total = [None] * outer
    for d in range(len(fresnels)):
        phase = (math.pi * fresnels[d]) * col_freq2
        col_cos, col_sin = jnp.cos(phase), jnp.sin(phase)
        row_phase = (math.pi * fresnels[d]) * row_freq2
        left_cos, left_sin = left[0] * jnp.cos(row_phase), left[1] * jnp.sin(row_phase)
        mix = dot(left_cos - left_sin, right)
        mix_back = dot(left_cos + left_sin, right)
        scaled = []
        for k in range(outer):
            c, s = col_cos[k : k + 1], col_sin[k : k + 1]
            re, im = spec_re[k], spec_im[k]
            scaled.append(jnp.concatenate([re * c + im * s, im * c - re * s], axis=1))
        parts = columns_inverse(jnp.concatenate(scaled, axis=0), inverse, mix_cos, mix_sin)
        stacked = jnp.concatenate([jnp.concatenate(part, axis=0) for part in parts], axis=1)
        field = dot(mix, stacked * (1.0 / width))
        re, im = field[:rows], field[rows:]
        slope_of = (re * re + im * im - measured[d]) * (4.0 / angles_total)
        back = dot(mix_back, jnp.concatenate([slope_of * re, slope_of * im], axis=0))
        pieces = [
            (back[:rows, q * LANES : (q + 1) * LANES], back[rows:, q * LANES : (q + 1) * LANES])
            for q in range(outer)
        ]
        adjoint = columns_forward(pieces, forward, mix_cos, mix_sin)
        for k in range(outer):
            c, s = col_cos[k : k + 1], col_sin[k : k + 1]
            re = adjoint[k * rows : (k + 1) * rows, :LANES]
            im = adjoint[k * rows : (k + 1) * rows, LANES:]
            term = jnp.concatenate([re * c - im * s, im * c + re * s], axis=1)
            total[k] = term if total[k] is None else total[k] + term
    parts = columns_inverse(jnp.concatenate(total, axis=0), inverse, mix_cos, mix_sin)
    grads = []
    for q in range(outer):
        (re, im), (wave_re, wave_im) = parts[q], waves[q]
        re, im = re * (1.0 / width), im * (1.0 / width)
        grads.append(re * (-ABSORB * wave_re - wave_im) + im * (wave_re - ABSORB * wave_im))
    result = []
    for a in range(angles):
        own = [g[a * slices : (a + 1) * slices] * scales[a] for g in grads]
        result.append(band_backward(own, steps[a]))
    return result


def image_kernel(
    angles, slices, outer, angles_total,
    slope_ref, fresnel_ref, other_fresnel_ref, own_ref, other_ref, ray_ref,
    forward_ref, inverse_ref, small_ref, left_ref, right_ref, freq_ref, out_ref,
):
    stride = 2 * angles * outer
    rays = []
    for a in range(angles):
        rays.append([
            ray_ref[pl.ds(a * outer + q, slices, stride), :]
            + ray_ref[pl.ds((angles + a) * outer + q, slices, stride), :]
            for q in range(outer)
        ])
    rows = angles * slices
    tables = (
        forward_ref[...], inverse_ref[...], (small_ref[0], small_ref[1], small_ref[2]),
        (left_ref[0], left_ref[1]), right_ref[...], freq_ref[...],
    )
    result = image_step(
        rays, [slope_ref[a] for a in range(angles)], [fresnel_ref[0], other_fresnel_ref[0]],
        [own_ref[...].reshape(rows, outer * LANES), other_ref[...].reshape(rows, outer * LANES)],
        tables, angles_total,
    )
    for a in range(angles):
        for q in range(outer):
            for copy in range(2):
                out_ref[pl.ds((copy * angles + a) * outer + q, slices, stride), :] = result[a][q]


def image_call(slopes, fresnel, other_fresnel, own, other, rays, angles_total):
    angles, slices, width = own.shape
    outer = width // LANES
    tables = column_tables(width) + row_tables(slices, angles)
    smem = pl.BlockSpec(memory_space=pltpu.SMEM)
    vmem = pl.BlockSpec(memory_space=pltpu.VMEM)
    return pl.pallas_call(
        partial(image_kernel, angles, slices, outer, angles_total),
        out_shape=jax.ShapeDtypeStruct(rays.shape, jnp.float32),
        in_specs=[smem] * 3 + [vmem] * 9,
        out_specs=vmem,
        compiler_params=pltpu.CompilerParams(vmem_limit_bytes=48 * 2**20),
    )(slopes, fresnel, other_fresnel, own, other, rays, *[jnp.asarray(t) for t in tables])


def shards(volume, row_weights, angle_slope, shear_index, shear_weight, fresnel, measured):
    row_count, width = volume.shape[1], volume.shape[2]
    angles_total = row_weights.shape[0]
    group, slices = measured.shape[1], measured.shape[2]
    angles = group // 2
    outer = width // LANES
    both = ("ang", "dist")
    dist = lax.axis_index("dist")
    mine = (lax.axis_index("ang") * 2 + dist) * angles
    swap = [(0, 1), (1, 0)]
    own = lax.dynamic_slice_in_dim(measured[0], dist * angles, angles, 0)
    other = lax.ppermute(
        lax.dynamic_slice_in_dim(measured[0], (1 - dist) * angles, angles, 0), "dist", swap
    )
    other_fresnel = lax.ppermute(fresnel, "dist", swap)
    slopes = lax.dynamic_slice_in_dim(angle_slope, mine, angles, 0)
    own_weights = lax.dynamic_slice_in_dim(row_weights, dist * row_count, row_count, 1)
    rays = jnp.einsum("ay,yx->ax", own_weights, volume[0], precision=HIGHEST)
    rays = lax.all_to_all(rays.reshape(angles_total, outer, LANES), both, 0, 0, tiled=True)
    spread = image_call(
        slopes, fresnel, other_fresnel, own, other, rays.reshape(-1, LANES), angles_total
    )
    spread = lax.all_to_all(spread.reshape(angles_total, outer, LANES), both, 0, 0, tiled=True)
    spread = spread.reshape(angles_total, width)
    return jnp.einsum("ay,ax->yx", own_weights, spread, precision=HIGHEST)[None]


def solution(mesh):
    placed = (P("ang", "dist", None), P(), P(), P(), P(), P("dist"), P("dist", "ang", None, None))
    return jax.shard_map(
        shards, mesh=mesh, in_specs=placed, out_specs=P("ang", "dist", None), check_vma=False
    )
```

time: 2100 us -> 46.5 us (0.02)
  local copies, waits for them, and re-layouts: 1040 us -> 2.98 us
  other arithmetic: 927 us -> 0 us
  waiting for transfers between devices: 87.5 us -> 8.19 us
    gather x2 -> x0, local copies, waits for them, and re-layouts: 1040 us -> none  [the longest x1 518 us: resample(): lower_tap = jnp.take_along_axis(rays, lower_index, axis=2)]
    unnamed x6 -> x0, other arithmetic: 905 us -> none
    all_gather x1 -> x0, waiting for transfers between devices: 49.8 us -> none  [shards(): lax.all_gather(volume, 'dist', axis=1, tiled=True)]
  transfers between devices with their start and end apart: 4 -> 3, of which waited for: 4 -> 2; matrix products, arithmetic and copies ran while one was open for 1% -> 0% of each run, Pallas kernels for 0% -> 0%
where the time goes in v1:
time: 46.5 us; the launch traced here: 45.9 us
  blocking collectives  13.1 us (28%)
  starting transfers between devices  8.63 us (19%)
  waiting for transfers between devices  8.19 us (18%)
  Pallas kernels  6.89 us (15%)
  matrix products  5.29 us (11%)
  local copies, waits for them, and re-layouts  2.98 us (6%)
  between operations  0.85 us (2%)
    all_to_all x1, blocking collectives, shards(): lax.all_to_all(spread.reshape(angles_total, outer, LANES), both, 0, 0, ti...  13.1 us
    all_to_all x1, starting transfers between devices, shards(): lax.all_to_all(rays.reshape(angles_total, outer, LANES), both, 0, 0, tile...  7.1 us
    pallas_call x1, Pallas kernels, image_call(): pl.pallas_call(partial(image_kernel, angles, slices, outer, angles_total)...  6.89 us
    ppermute x1, waiting for transfers between devices, shards(): other_fresnel = lax.ppermute(fresnel, 'dist', swap)  4.97 us
    all_to_all x1, waiting for transfers between devices, shards(): lax.all_to_all(rays.reshape(angles_total, outer, LANES), both, 0, 0, tile...  3.21 us
    dot_general x1, matrix products, shards(): return jnp.einsum('ay,ax->yx', own_weights, spread, precision=HIGHEST)[None]  3.16 us
    dot_general x2, local copies, waits for them, and re-layouts, shards(): rays = jnp.einsum('ay,yx->ax', own_weights, volume[0], precision=HIGHEST)  2.83 us
    dot_general x1, matrix products, shards(): rays = jnp.einsum('ay,yx->ax', own_weights, volume[0], precision=HIGHEST)  2.13 us
  transfers between devices with their start and end apart: 3, of which 2 were waited for; matrix products, arithmetic and copies ran while one was open for 0% of the time, Pallas kernels for 0%

profile of v1, /device:TPU:1, one launch (start us, length us, event | category | flops | bytes accessed | tf_op | source)
XLA Modules:
  0.0 45.9 jit_solution(10753203052680865949)
XLA Ops:
  0.0 0.0 copy-start
  0.0 2.0 %copy.16 = f32[1024,512]{1,0:T(8,128)S(1)} copy(f32[1024,512]{0,1:T(8,128)} %bitcast.23) | data formatting | bytes 4194304 | tf_op jit(solution)/shard_map/ay,yx->ax/dot_general | solution.py:293
  2.0 0.0 copy-start.7
  2.0 0.0 copy-start.8
  2.0 0.0 copy-start.1
  2.0 0.0 copy-start.2
  2.0 0.0 copy-start.3
  2.0 0.0 copy-start.4
  2.0 0.0 copy-start.5
  2.1 0.0 copy-start.6
  2.1 0.0 copy-done
  2.1 2.1 %fusion.2 = f32[64,8,128]{2,0,1:T(8,128)S(1)} fusion(f32[8,128,512]{2,1,0:T(8,128)S(1)} %bitcast.22, f32[64,1024]{1,0:T(8,128)S(1)} %copy-done, s32[]{:T(128)S(6)} %select_n.12), kind=kOutput, calls=%fused_computation.3 | convolution fusion | flops 402653184 | bytes 2490372 | tf_op jit(solution)/shard_map/ay,yx->ax/dot_general | solution.py:293
  4.2 0.9 %copy.15 = f32[64,8,128]{2,1,0:T(8,128)} copy(f32[64,8,128]{2,0,1:T(8,128)S(1)} %fusion.2) | data formatting | bytes 524288 | tf_op jit(solution)/shard_map/ay,yx->ax/dot_general | solution.py:293
  5.1 7.1 %all-to-all-start = ((f32[64,8,128]{2,1,0:T(8,128)}), f32[64,8,128]{2,1,0:T(8,128)S(1)}, u32[]{:S(2)}, u32[]{:S(2)}) async-start(f32[64,8,128]{2,1,0:T(8,128)} %copy.15), calls=%async_computation | async-start | bytes 524288 | tf_op jit(solution)/shard_map/all_to_all | solution.py:294
  12.2 0.0 copy-done.7
  12.2 1.5 %collective-permute-start.1 = (f32[2,16,1024]{2,1,0:T(8,128)S(1)}, f32[2,16,1024]{2,1,0:T(8,128)S(1)}, u32[]{:S(2)}, u32[]{:S(2)}) collective-permute-start(f32[2,16,1024]{2,1,0:T(8,128)S(1)} %get-tuple-element.5), channel_id=1, source_target_pairs={{0,1},{1,0},{2,3},{3,2},{4,5},{5,4},{6,7},{7,6},{8,9},{9,8},{10,11... | collective-permute-start | bytes 393224 | tf_op jit(solution)/shard_map/ppermute | solution.py:287
  13.7 0.1 collective-permute-start
  14.5 0.0 copy-done.8
  14.5 0.1 dynamic_slice.17.slope_ref
  14.5 5.0 %collective-permute-done.other_fresnel_ref = f32[1]{0:T(128)} collective-permute-done((f32[1]{0:T(128)}, f32[1]{0:T(128)}, u32[]{:S(2)}, u32[]{:S(2)}) %collective-permute-start) | collective-permute-done | bytes 36 | tf_op jit(solution)/shard_map/ppermute | solution.py:290
  19.5 0.0 collective-permute-done.1.other_ref
  19.5 3.2 %all-to-all-done = f32[64,8,128]{2,1,0:T(8,128)S(1)} async-done(((f32[64,8,128]{2,1,0:T(8,128)}), f32[64,8,128]{2,1,0:T(8,128)S(1)}, u32[]{:S(2)}, u32[]{:S(2)}) %all-to-all-start) | async-done | bytes 262176 | tf_op jit(solution)/shard_map/all_to_all | solution.py:294
  22.7 0.0 copy-done.1
  22.7 0.0 copy-done.2
  22.7 0.0 copy-done.3
  22.7 0.0 copy-done.4
  22.8 0.0 copy-done.5
  22.8 0.0 copy-done.6
  22.8 6.9 %shard_map.109 = f32[512,128]{1,0:T(8,128)S(1)} custom-call(s32[2]{0:T(128)S(1)} %dynamic_slice.17.slope_ref, f32[1]{0:T(128)S(6)} %copy.22.fresnel_ref, f32[1]{0:T(128)} %collective-permute-done.other_fresnel_ref, f32[2,16,1024]{2,1,0:T(8,128)S(1)} %get-tuple-element.6.own_ref, f32[2,16,1024]{2,1,0:T(8,128)S(1)} %collective-permute-done.1.other_ref, ...), custom_call_target="tpu_custom_call" | custom-call | tf_op jit(solution)/shard_map/pallas_call | solution.py:267
  29.7 13.1 %all_to_all.10 = f32[64,8,128]{2,1,0:T(8,128)S(1)} all-to-all(f32[64,8,128]{2,1,0:T(8,128)S(1)} %bitcast.21), channel_id=1, replica_groups=mesh['ang'=16,'dist'=2] {'ang','dist'}, dimensions={0} | all-to-all | bytes 524288 | tf_op jit(solution)/shard_map/all_to_all | solution.py:298
  42.8 3.2 %convolution_bitcast_fusion = f32[1,512,1024]{2,1,0:T(8,128)} fusion(f32[8,8,8,128]{3,2,1,0:T(8,128)S(1)} %bitcast.24, f32[64,1024]{1,0:T(8,128)S(1)} %copy-done, s32[]{:T(128)S(6)} %select_n.12), kind=kOutput, calls=%fused_computation | convolution fusion | flops 402653184 | bytes 2490372 | tf_op jit(solution)/shard_map/ay,ax->yx/dot_general | solution.py:300
  (1 shorter events, 0.0 us)
Async XLA Ops:
  0.0 2.1 %copy-start = (f32[64,1024]{1,0:T(8,128)S(1)}, f32[64,1024]{1,0:T(8,128)}, u32[]{:S(2)}) copy-start(f32[64,1024]{1,0:T(8,128)} %param.14) | copy-start | bytes 786436
  2.0 10.2 %copy-start.7 = (f32[1,4,16,1024]{3,2,1,0:T(8,128)S(1)}, f32[1,4,16,1024]{3,2,1,0:T(8,128)}, u32[]{:S(2)}) copy-start(f32[1,4,16,1024]{3,2,1,0:T(8,128)} %param.17) | copy-start | bytes 786436
  2.0 12.5 %copy-start.8 = (s32[64]{0:T(128)S(1)}, s32[64]{0:T(128)}, u32[]{:S(2)}) copy-start(s32[64]{0:T(128)} %param.15) | copy-start | bytes 772
  2.0 20.7 %copy-start.1 = (f32[256,256]{1,0:T(8,128)S(1)}, f32[256,256]{1,0:T(8,128)}, u32[]{:S(2)}) copy-start(f32[256,256]{1,0:T(8,128)} %constant.36.clone.forward_ref) | copy-start | bytes 786436
  2.0 20.7 %copy-start.2 = (f32[256,256]{1,0:T(8,128)S(1)}, f32[256,256]{1,0:T(8,128)}, u32[]{:S(2)}) copy-start(f32[256,256]{1,0:T(8,128)} %constant.37.clone.inverse_ref) | copy-start | bytes 786436
  2.0 20.7 %copy-start.3 = (f32[2,64,128]{2,1,0:T(8,128)S(1)}, f32[2,64,128]{2,1,0:T(8,128)}, u32[]{:S(2)}) copy-start(f32[2,64,128]{2,1,0:T(8,128)} %constant.39.clone.left_ref) | copy-start | bytes 196612
  2.0 20.7 %copy-start.4 = (f32[128,64]{1,0:T(8,128)S(1)}, f32[128,64]{1,0:T(8,128)}, u32[]{:S(2)}) copy-start(f32[128,64]{1,0:T(8,128)} %constant.40.clone.right_ref) | copy-start | bytes 98308
  2.0 20.7 %copy-start.5 = (f32[3,8,128]{2,1,0:T(8,128)S(1)}, f32[3,8,128]{2,1,0:T(8,128)}, u32[]{:S(2)}) copy-start(f32[3,8,128]{2,1,0:T(8,128)} %constant.38.clone.small_ref) | copy-start | bytes 36868
  2.1 20.7 %copy-start.6 = (f32[1,128]{1,0:T(1,128)S(1)}, f32[1,128]{1,0:T(1,128)}, u32[]{:S(2)}) copy-start(f32[1,128]{1,0:T(1,128)} %constant.41.clone.freq_ref) | copy-start | bytes 1540
  5.1 17.7 %all-to-all-start = ((f32[64,8,128]{2,1,0:T(8,128)}), f32[64,8,128]{2,1,0:T(8,128)S(1)}, u32[]{:S(2)}, u32[]{:S(2)}) async-start(f32[64,8,128]{2,1,0:T(8,128)} %copy.15), calls=%async_computation | async-start | bytes 524288 | tf_op jit(solution)/shard_map/all_to_all | solution.py:294
  12.2 7.3 %collective-permute-start.1 = (f32[2,16,1024]{2,1,0:T(8,128)S(1)}, f32[2,16,1024]{2,1,0:T(8,128)S(1)}, u32[]{:S(2)}, u32[]{:S(2)}) collective-permute-start(f32[2,16,1024]{2,1,0:T(8,128)S(1)} %get-tuple-element.5), channel_id=1, source_target_pairs={{0,1},{1,0},{2,3},{3,2},{4,5},{5,4},{6,7},{7,6},{8,9},{9,8},{10,11... | collective-permute-start | bytes 393224 | tf_op jit(solution)/shard_map/ppermute | solution.py:287
  13.7 5.8 %collective-permute-start = (f32[1]{0:T(128)}, f32[1]{0:T(128)}, u32[]{:S(2)}, u32[]{:S(2)}) collective-permute-start(f32[1]{0:T(128)} %param.16), channel_id=1, source_target_pairs={{0,1},{1,0},{2,3},{3,2},{4,5},{5,4},{6,7},{7,6},{8,9},{9,8},{10,11... | collective-permute-start | bytes 20 | tf_op jit(solution)/shard_map/ppermute | solution.py:290

commit v2 on v1

--- a/solution.py
+++ b/solution.py
@@ -229,74 +229,159 @@
     return result
 
 
-def image_kernel(
-    angles, slices, outer, angles_total,
-    slope_ref, fresnel_ref, other_fresnel_ref, own_ref, other_ref, ray_ref,
+def fused_kernel(
+    sizes, slope_ref, fresnel_ref, volume_hbm, weight_ref, measured_hbm,
     forward_ref, inverse_ref, small_ref, left_ref, right_ref, freq_ref, out_ref,
+    volume_ref, own_ref, other_ref, fresnel_out, fresnel_in, send_ref, recv_ref, back_ref,
+    local_sem, swap_send, swap_recv, send_sem, recv_sem, back_send, back_recv,
 ):
-    stride = 2 * angles * outer
+    angles, slices, outer, angles_total, rows_own, devices = sizes
+    ang, dist = lax.axis_index("ang"), lax.axis_index("dist")
+    me = ang * 2 + dist
+    piece = angles * outer
+    rows = angles * slices
+    barrier = pltpu.get_barrier_semaphore()
+
+    def place_of(step):
+        there = lax.rem(me + step, devices)
+        return there, (there // 2, lax.rem(there, 2))
+
+    volume_copy = pltpu.make_async_copy(volume_hbm, volume_ref, local_sem.at[0])
+    volume_copy.start()
+    own_copy = pltpu.make_async_copy(
+        measured_hbm.at[pl.ds(dist * angles, angles)], own_ref, local_sem.at[1]
+    )
+    own_copy.start()
+
+    def greet(step, carry):
+        pl.semaphore_signal(
+            barrier, inc=1, device_id=place_of(step)[1], device_id_type=pl.DeviceIdType.MESH
+        )
+        return carry
+
+    lax.fori_loop(1, devices, greet, 0)
+    fresnel_out[...] = jnp.full(fresnel_out.shape, fresnel_ref[0])
+    weights = weight_ref[:, pl.ds(pl.multiple_of(dist * rows_own, LANES), rows_own)]
+    volume_copy.wait()
+    for q in range(outer):
+        send_ref[pl.ds(q, angles_total, outer), :] = dot(
+            weights, volume_ref[:, q * LANES : (q + 1) * LANES]
+        )
+    pl.semaphore_wait(barrier, devices - 1)
+
+    def send(step, carry):
+        there, target = place_of(step)
+        pltpu.make_async_remote_copy(
+            src_ref=send_ref.at[pl.ds(there * piece, piece)],
+            dst_ref=recv_ref.at[pl.ds(me * piece, piece)],
+            send_sem=send_sem, recv_sem=recv_sem,
+            device_id=target, device_id_type=pl.DeviceIdType.MESH,
+        ).start()
+        return carry
+
+    lax.fori_loop(1, devices, send, 0)
+    pltpu.make_async_copy(
+        send_ref.at[pl.ds(me * piece, piece)], recv_ref.at[pl.ds(me * piece, piece)], recv_sem
+    ).start()
+    swaps = []
+    for n, (source, target) in enumerate((
+        (fresnel_out, fresnel_in),
+        (measured_hbm.at[pl.ds((1 - dist) * angles, angles)], other_ref),
+    )):
+        swaps.append(pltpu.make_async_remote_copy(
+            src_ref=source, dst_ref=target, send_sem=swap_send.at[n], recv_sem=swap_recv.at[n],
+            device_id=(ang, 1 - dist), device_id_type=pl.DeviceIdType.MESH,
+        ))
+        swaps[n].start()
+    own_copy.wait()
+    for swap in swaps:
+        swap.wait()
+    fresnels = [fresnel_out[0:1, 0:1], fresnel_in[0:1, 0:1]]
+    shift = devices - 1
+    pltpu.make_async_copy(recv_ref, recv_ref, recv_sem).wait()
+    part = send_ref.at[pl.ds(0, shift * piece)]
+    pltpu.make_async_copy(part, part, send_sem).wait()
+    stride = 2 * piece
     rays = []
     for a in range(angles):
         rays.append([
-            ray_ref[pl.ds(a * outer + q, slices, stride), :]
-            + ray_ref[pl.ds((angles + a) * outer + q, slices, stride), :]
+            recv_ref[pl.ds(a * outer + q, slices, stride), :]
+            + recv_ref[pl.ds((angles + a) * outer + q, slices, stride), :]
             for q in range(outer)
         ])
-    rows = angles * slices
     tables = (
         forward_ref[...], inverse_ref[...], (small_ref[0], small_ref[1], small_ref[2]),
         (left_ref[0], left_ref[1]), right_ref[...], freq_ref[...],
     )
     result = image_step(
-        rays, [slope_ref[a] for a in range(angles)], [fresnel_ref[0], other_fresnel_ref[0]],
+        rays, [slope_ref[me * angles + a] for a in range(angles)], fresnels,
         [own_ref[...].reshape(rows, outer * LANES), other_ref[...].reshape(rows, outer * LANES)],
         tables, angles_total,
     )
     for a in range(angles):
         for q in range(outer):
-            for copy in range(2):
-                out_ref[pl.ds((copy * angles + a) * outer + q, slices, stride), :] = result[a][q]
-
-
-def image_call(slopes, fresnel, other_fresnel, own, other, rays, angles_total):
-    angles, slices, width = own.shape
-    outer = width // LANES
+            back_ref[pl.ds(a * outer + q, slices, piece), :] = result[a][q]
+
+    def send_back(step, carry):
+        there, target = place_of(step)
+        pltpu.make_async_remote_copy(
+            src_ref=back_ref.at[pl.ds((there // 2) * piece, piece)],
+            dst_ref=out_ref.at[pl.ds(me * piece, piece)],
+            send_sem=back_send, recv_sem=back_recv,
+            device_id=target, device_id_type=pl.DeviceIdType.MESH,
+        ).start()
+        return carry
+
+    lax.fori_loop(1, devices, send_back, 0)
+    pltpu.make_async_copy(
+        back_ref.at[pl.ds(ang * piece, piece)], out_ref.at[pl.ds(me * piece, piece)], back_recv
+    ).start()
+    pltpu.make_async_copy(out_ref, out_ref, back_recv).wait()
+    sent = out_ref.at[pl.ds(0, shift * piece)]
+    pltpu.make_async_copy(sent, sent, back_send).wait()
+
+
+def fused_call(slopes, fresnel, volume, weights, measured):
+    group, slices, width = measured.shape
+    angles, outer = group // 2, width // LANES
+    angles_total, rows_own = weights.shape[0], volume.shape[0]
+    devices = angles_total // angles
+    piece = angles * outer
     tables = column_tables(width) + row_tables(slices, angles)
     smem = pl.BlockSpec(memory_space=pltpu.SMEM)
     vmem = pl.BlockSpec(memory_space=pltpu.VMEM)
+    hbm = pl.BlockSpec(memory_space=pl.ANY)
+    f32 = jnp.float32
+    dma = pltpu.SemaphoreType.DMA
     return pl.pallas_call(
-        partial(image_kernel, angles, slices, outer, angles_total),
-        out_shape=jax.ShapeDtypeStruct(rays.shape, jnp.float32),
-        in_specs=[smem] * 3 + [vmem] * 9,
+        partial(fused_kernel, (angles, slices, outer, angles_total, rows_own, devices)),
+        out_shape=jax.ShapeDtypeStruct((devices * piece, LANES), f32),
+        in_specs=[smem, smem, hbm, vmem, hbm] + [vmem] * 6,
         out_specs=vmem,
-        compiler_params=pltpu.CompilerParams(vmem_limit_bytes=48 * 2**20),
-    )(slopes, fresnel, other_fresnel, own, other, rays, *[jnp.asarray(t) for t in tables])
+        scratch_shapes=[
+            pltpu.VMEM((rows_own, width), f32),
+            pltpu.VMEM((angles, slices, width), f32),
+            pltpu.VMEM((angles, slices, width), f32),
+            pltpu.VMEM((8, LANES), f32),
+            pltpu.VMEM((8, LANES), f32),
+            pltpu.VMEM((devices * piece, LANES), f32),
+            pltpu.VMEM((devices * piece, LANES), f32),
+            pltpu.VMEM((slices * piece, LANES), f32),
+            dma((2,)), dma((2,)), dma((2,)), dma, dma, dma, dma,
+        ],
+        compiler_params=pltpu.CompilerParams(
+            vmem_limit_bytes=40 * 2**20, collective_id=0, has_side_effects=True
+        ),
+    )(slopes, fresnel, volume, weights, measured, *[jnp.asarray(t) for t in tables])
 
 
 def shards(volume, row_weights, angle_slope, shear_index, shear_weight, fresnel, measured):
     row_count, width = volume.shape[1], volume.shape[2]
-    angles_total = row_weights.shape[0]
-    group, slices = measured.shape[1], measured.shape[2]
-    angles = group // 2
-    outer = width // LANES
-    both = ("ang", "dist")
-    dist = lax.axis_index("dist")
-    mine = (lax.axis_index("ang") * 2 + dist) * angles
-    swap = [(0, 1), (1, 0)]
-    own = lax.dynamic_slice_in_dim(measured[0], dist * angles, angles, 0)
-    other = lax.ppermute(
-        lax.dynamic_slice_in_dim(measured[0], (1 - dist) * angles, angles, 0), "dist", swap
-    )
-    other_fresnel = lax.ppermute(fresnel, "dist", swap)
-    slopes = lax.dynamic_slice_in_dim(angle_slope, mine, angles, 0)
-    own_weights = lax.dynamic_slice_in_dim(row_weights, dist * row_count, row_count, 1)
-    rays = jnp.einsum("ay,yx->ax", own_weights, volume[0], precision=HIGHEST)
-    rays = lax.all_to_all(rays.reshape(angles_total, outer, LANES), both, 0, 0, tiled=True)
-    spread = image_call(
-        slopes, fresnel, other_fresnel, own, other, rays.reshape(-1, LANES), angles_total
-    )
-    spread = lax.all_to_all(spread.reshape(angles_total, outer, LANES), both, 0, 0, tiled=True)
-    spread = spread.reshape(angles_total, width)
+    own_weights = lax.dynamic_slice_in_dim(
+        row_weights, lax.axis_index("dist") * row_count, row_count, 1
+    )
+    spread = fused_call(angle_slope, fresnel, volume[0], row_weights, measured[0])
+    spread = spread.reshape(row_weights.shape[0], width)
     return jnp.einsum("ay,ax->yx", own_weights, spread, precision=HIGHEST)[None]
 
 

time: 46.5 us -> 40.8 us (0.88)
  Pallas kernels: 6.89 us -> 27.4 us
  blocking collectives: 13.1 us -> 0 us
  starting transfers between devices: 8.63 us -> 0 us
  waiting for transfers between devices: 8.19 us -> 0 us
  local copies, waits for them, and re-layouts: 2.98 us -> 9.13 us
  matrix products: 5.29 us -> 3.17 us
    pallas_call x1, Pallas kernels: 6.89 us -> 27.4 us  [fused_call(): pl.pallas_call(partial(fused_kernel, (angles, slices, outer, angles_total...]
    all_to_all x1 -> x0, blocking collectives: 13.1 us -> none  [shards(): lax.all_to_all(spread.reshape(angles_total, outer, LANES), both, 0, 0, ti...]
    unnamed x18 -> x22, local copies, waits for them, and re-layouts: 0.06 us -> 9.08 us
    all_to_all x1 -> x0, starting transfers between devices: 7.1 us -> none  [shards(): lax.all_to_all(rays.reshape(angles_total, outer, LANES), both, 0, 0, tile...]
    ppermute x2 -> x0, waiting for transfers between devices: 4.98 us -> none  [the longest x1 4.97 us: shards(): other_fresnel = lax.ppermute(fresnel, 'dist', swap)]
    all_to_all x1 -> x0, waiting for transfers between devices: 3.21 us -> none  [shards(): lax.all_to_all(rays.reshape(angles_total, outer, LANES), both, 0, 0, tile...]
    dot_general x2 -> x0, local copies, waits for them, and re-layouts: 2.83 us -> none  [shards(): rays = jnp.einsum('ay,yx->ax', own_weights, volume[0], precision=HIGHEST)]
    dot_general x1 -> x0, matrix products: 2.13 us -> none  [shards(): rays = jnp.einsum('ay,yx->ax', own_weights, volume[0], precision=HIGHEST)]
  transfers between devices with their start and end apart: 3 -> 0, of which waited for: 2 -> 0; matrix products, arithmetic and copies ran while one was open for 0% -> 0% of each run, Pallas kernels for 0% -> 0%
where the time goes in v2:
time: 40.8 us; the launch traced here: 40.4 us
  Pallas kernels  27.4 us (67%)
  local copies, waits for them, and re-layouts  9.13 us (22%)
  matrix products  3.17 us (8%)
  between operations  0.69 us (2%)
    pallas_call x1, Pallas kernels, fused_call(): pl.pallas_call(partial(fused_kernel, (angles, slices, outer, angles_total...  27.4 us
    unnamed x22, local copies, waits for them, and re-layouts  9.08 us
    dot_general x1, matrix products, shards(): return jnp.einsum('ay,ax->yx', own_weights, spread, precision=HIGHEST)[None]  3.17 us

profile of v2, /device:TPU:1, one launch (start us, length us, event | category | flops | bytes accessed | tf_op | source)
XLA Modules:
  0.0 40.4 jit_solution(9382740204312426499)
XLA Ops:
  0.7 0.0 copy-start
  0.7 1.6 %copy-done = f32[1,512,1024]{2,1,0:T(8,128)S(1)} copy-done((f32[1,512,1024]{2,1,0:T(8,128)S(1)}, f32[1,512,1024]{2,1,0:T(8,128)}, u32[]{:S(2)}) %copy-start) | copy-done | bytes 2097176
  2.2 0.0 copy-start.1
  2.2 0.9 %copy-done.1 = f32[64,1024]{1,0:T(8,128)S(1)} copy-done((f32[64,1024]{1,0:T(8,128)S(1)}, f32[64,1024]{1,0:T(8,128)}, u32[]{:S(2)}) %copy-start.1) | copy-done | bytes 262168
  3.2 0.0 copy-start.3
  3.2 0.9 %copy-done.3 = f32[1,4,16,1024]{3,2,1,0:T(8,128)S(1)} copy-done((f32[1,4,16,1024]{3,2,1,0:T(8,128)S(1)}, f32[1,4,16,1024]{3,2,1,0:T(8,128)}, u32[]{:S(2)}) %copy-start.3) | copy-done | bytes 262168
  4.1 0.0 copy-start.4
  4.1 0.9 %copy-done.4 = f32[256,256]{1,0:T(8,128)S(1)} copy-done((f32[256,256]{1,0:T(8,128)S(1)}, f32[256,256]{1,0:T(8,128)}, u32[]{:S(2)}) %copy-start.4) | copy-done | bytes 262168
  5.1 0.0 copy-start.5
  5.1 0.9 %copy-done.5 = f32[256,256]{1,0:T(8,128)S(1)} copy-done((f32[256,256]{1,0:T(8,128)S(1)}, f32[256,256]{1,0:T(8,128)}, u32[]{:S(2)}) %copy-start.5) | copy-done | bytes 262168
  6.0 0.0 copy-start.6
  6.0 0.8 %copy-done.6 = f32[128,64]{1,0:T(8,128)S(1)} copy-done((f32[128,64]{1,0:T(8,128)S(1)}, f32[128,64]{1,0:T(8,128)}, u32[]{:S(2)}) %copy-start.6) | copy-done | bytes 32792
  6.9 0.0 copy-start.7
  6.9 0.8 %copy-done.7 = f32[2,64,128]{2,1,0:T(8,128)S(1)} copy-done((f32[2,64,128]{2,1,0:T(8,128)S(1)}, f32[2,64,128]{2,1,0:T(8,128)}, u32[]{:S(2)}) %copy-start.7) | copy-done | bytes 65560
  7.7 0.0 copy-start.8
  7.7 0.7 %copy-done.8 = f32[3,8,128]{2,1,0:T(8,128)S(1)} copy-done((f32[3,8,128]{2,1,0:T(8,128)S(1)}, f32[3,8,128]{2,1,0:T(8,128)}, u32[]{:S(2)}) %copy-start.8) | copy-done | bytes 12312
  8.4 0.0 copy-start.9
  8.4 0.7 %copy-done.9 = s32[64]{0:T(128)S(1)} copy-done((s32[64]{0:T(128)S(1)}, s32[64]{0:T(128)}, u32[]{:S(2)}) %copy-start.9) | copy-done | bytes 280
  9.1 0.0 copy-start.10
  9.1 0.7 %copy-done.10 = f32[1,128]{1,0:T(1,128)S(1)} copy-done((f32[1,128]{1,0:T(1,128)S(1)}, f32[1,128]{1,0:T(1,128)}, u32[]{:S(2)}) %copy-start.10) | copy-done | bytes 536
  9.7 0.0 copy-start.2
  9.7 27.4 %shard_map.109 = f32[512,128]{1,0:T(8,128)S(1)} custom-call(s32[64]{0:T(128)S(1)} %copy-done.9, f32[1]{0:T(128)S(6)} %copy.12.fresnel_ref, f32[512,1024]{1,0:T(8,128)S(1)} %bitcast.5, f32[64,1024]{1,0:T(8,128)S(1)} %copy-done.1, f32[4,16,1024]{2,1,0:T(8,128)S(1)} %bitcast.6, f32[256,256]{1,0:T(8,128)S(1)} %copy-done.5, f32[256,256]{1,0:T(8,128)S(1)} %copy-done.4, ...), custom_call_target="tpu_custom_call" | custom-call | tf_op jit(solution)/shard_map/pallas_call | solution.py:356
  37.2 0.0 copy-done.2
  37.2 3.2 %convolution_bitcast_fusion = f32[1,512,1024]{2,1,0:T(8,128)} fusion(f32[64,1024]{1,0:T(8,128)S(1)} %reshape.3, f32[64,1024]{1,0:T(8,128)S(1)} %copy-done.2, s32[]{:T(128)S(6)} %select_n.3), kind=kOutput, calls=%fused_computation | convolution fusion | flops 402653184 | bytes 2490372 | tf_op jit(solution)/shard_map/ay,ax->yx/dot_general | solution.py:385
  (1 shorter events, 0.0 us)
Async XLA Ops:
  0.7 1.6 %copy-start = (f32[1,512,1024]{2,1,0:T(8,128)S(1)}, f32[1,512,1024]{2,1,0:T(8,128)}, u32[]{:S(2)}) copy-start(f32[1,512,1024]{2,1,0:T(8,128)} %param.13) | copy-start | bytes 6291460
  2.2 0.9 %copy-start.1 = (f32[64,1024]{1,0:T(8,128)S(1)}, f32[64,1024]{1,0:T(8,128)}, u32[]{:S(2)}) copy-start(f32[64,1024]{1,0:T(8,128)} %weight_ref.1) | copy-start | bytes 786436
  3.2 0.9 %copy-start.3 = (f32[1,4,16,1024]{3,2,1,0:T(8,128)S(1)}, f32[1,4,16,1024]{3,2,1,0:T(8,128)}, u32[]{:S(2)}) copy-start(f32[1,4,16,1024]{3,2,1,0:T(8,128)} %param.17) | copy-start | bytes 786436
  4.1 0.9 %copy-start.4 = (f32[256,256]{1,0:T(8,128)S(1)}, f32[256,256]{1,0:T(8,128)}, u32[]{:S(2)}) copy-start(f32[256,256]{1,0:T(8,128)} %constant.23.clone.inverse_ref) | copy-start | bytes 786436
  5.1 0.9 %copy-start.5 = (f32[256,256]{1,0:T(8,128)S(1)}, f32[256,256]{1,0:T(8,128)}, u32[]{:S(2)}) copy-start(f32[256,256]{1,0:T(8,128)} %constant.22.clone.forward_ref) | copy-start | bytes 786436
  6.0 0.8 %copy-start.6 = (f32[128,64]{1,0:T(8,128)S(1)}, f32[128,64]{1,0:T(8,128)}, u32[]{:S(2)}) copy-start(f32[128,64]{1,0:T(8,128)} %constant.26.clone.right_ref) | copy-start | bytes 98308
  6.9 0.8 %copy-start.7 = (f32[2,64,128]{2,1,0:T(8,128)S(1)}, f32[2,64,128]{2,1,0:T(8,128)}, u32[]{:S(2)}) copy-start(f32[2,64,128]{2,1,0:T(8,128)} %constant.25.clone.left_ref) | copy-start | bytes 196612
  7.7 0.7 %copy-start.8 = (f32[3,8,128]{2,1,0:T(8,128)S(1)}, f32[3,8,128]{2,1,0:T(8,128)}, u32[]{:S(2)}) copy-start(f32[3,8,128]{2,1,0:T(8,128)} %constant.24.clone.small_ref) | copy-start | bytes 36868
  8.4 0.7 %copy-start.9 = (s32[64]{0:T(128)S(1)}, s32[64]{0:T(128)}, u32[]{:S(2)}) copy-start(s32[64]{0:T(128)} %slope_ref.1) | copy-start | bytes 772
  9.1 0.7 %copy-start.10 = (f32[1,128]{1,0:T(1,128)S(1)}, f32[1,128]{1,0:T(1,128)}, u32[]{:S(2)}) copy-start(f32[1,128]{1,0:T(1,128)} %constant.27.clone.freq_ref) | copy-start | bytes 1540
  9.7 27.5 %copy-start.2 = (f32[64,1024]{1,0:T(8,128)S(1)}, f32[64,1024]{1,0:T(8,128)}, u32[]{:S(2)}) copy-start(f32[64,1024]{1,0:T(8,128)} %weight_ref.1) | copy-start | bytes 786436

commit v3 on v2

--- a/solution.py
+++ b/solution.py
@@ -20,6 +20,29 @@
     )
 
 
+def dot_narrow(a, b):
+    return lax.dot_general(a, b, (((1,), (0,)), ((), ())), preferred_element_type=jnp.float32)
+
+
+def halves(a):
+    high = a.astype(jnp.bfloat16)
+    return high, (a - high.astype(jnp.float32)).astype(jnp.bfloat16)
+
+
+def dot_left(a, high, low):
+    rows = a.shape[0]
+    a_high, a_low = halves(a)
+    both = dot_narrow(jnp.concatenate([a_high, a_low], axis=0), high)
+    return both[:rows] + both[rows:] + dot_narrow(a_high, low)
+
+
+def dot_right(table, table_high, b):
+    rows = table_high.shape[0]
+    b_high, b_low = halves(b)
+    both = dot_narrow(table, b_high)
+    return both[:rows] + both[rows:] + dot_narrow(table_high, b_low)
+
+
 def signed_freq(counter, length):
     return np.where(counter <= (length - 1) // 2, counter, counter - length) / length
 
@@ -31,11 +54,12 @@
     ang = 2 * np.pi * (p[:, None] * p[None, :] % LANES) / LANES
     c, s = np.cos(ang), np.sin(ang)
     forward = np.block([[c, -s], [s, c]])
-    inverse = np.block([[c, s], [-s, c]])
+    high = forward.astype(jnp.bfloat16)
+    low = (forward - high.astype(np.float64)).astype(jnp.bfloat16)
     mixed = 2 * np.pi * (k[:, None] * p[None, :] % width) / width
     freq2 = signed_freq(k[:, None] + outer * p[None, :], width) ** 2
     small = np.stack([np.cos(mixed), np.sin(mixed), freq2])
-    return forward.astype(np.float32), inverse.astype(np.float32), small.astype(np.float32)
+    return np.stack([high, low]), small.astype(np.float32)
 
 
 def row_tables(slices, angles):
@@ -85,17 +109,17 @@
     for k, (re, im) in enumerate(parts):
         c, s = mix_cos[k : k + 1], mix_sin[k : k + 1]
         rows.append(jnp.concatenate([re * c + im * s, im * c - re * s], axis=1))
-    return dot(jnp.concatenate(rows, axis=0), table)
+    return dot_left(jnp.concatenate(rows, axis=0), *table)
 
 
 def columns_inverse(spectrum, table, mix_cos, mix_sin):
     outer = mix_cos.shape[0]
     count = spectrum.shape[0] // outer
-    result = dot(spectrum, table)
+    result = dot_left(spectrum, *table)
     parts = []
     for k in range(outer):
-        re = result[k * count : (k + 1) * count, :LANES]
-        im = result[k * count : (k + 1) * count, LANES:]
+        im = result[k * count : (k + 1) * count, :LANES]
+        re = result[k * count : (k + 1) * count, LANES:]
         c, s = mix_cos[k : k + 1], mix_sin[k : k + 1]
         parts.append((re * c - im * s, im * c + re * s))
     return fft_list(parts, 1)
@@ -165,7 +189,7 @@
 
 
 def image_step(ray_tiles, slopes, fresnels, measured, tables, angles_total):
-    forward, inverse, small, left, right, row_freq2 = tables
+    forward, small, left, right, row_freq2 = tables
     angles, outer = len(ray_tiles), len(ray_tiles[0])
     slices = ray_tiles[0][0].shape[0]
     rows = angles * slices
@@ -192,19 +216,19 @@
         col_cos, col_sin = jnp.cos(phase), jnp.sin(phase)
         row_phase = (math.pi * fresnels[d]) * row_freq2
         left_cos, left_sin = left[0] * jnp.cos(row_phase), left[1] * jnp.sin(row_phase)
-        mix = dot(left_cos - left_sin, right)
-        mix_back = dot(left_cos + left_sin, right)
+        mix = jnp.concatenate(halves(dot(left_cos - left_sin, right)), axis=0)
+        mix_back = jnp.concatenate(halves(dot(left_cos + left_sin, right)), axis=0)
         scaled = []
         for k in range(outer):
             c, s = col_cos[k : k + 1], col_sin[k : k + 1]
             re, im = spec_re[k], spec_im[k]
-            scaled.append(jnp.concatenate([re * c + im * s, im * c - re * s], axis=1))
-        parts = columns_inverse(jnp.concatenate(scaled, axis=0), inverse, mix_cos, mix_sin)
+            scaled.append(jnp.concatenate([im * c - re * s, re * c + im * s], axis=1))
+        parts = columns_inverse(jnp.concatenate(scaled, axis=0), forward, mix_cos, mix_sin)
         stacked = jnp.concatenate([jnp.concatenate(part, axis=0) for part in parts], axis=1)
-        field = dot(mix, stacked * (1.0 / width))
+        field = dot_right(mix, mix[: 2 * rows], stacked * (1.0 / width))
         re, im = field[:rows], field[rows:]
         slope_of = (re * re + im * im - measured[d]) * (4.0 / angles_total)
-        back = dot(mix_back, jnp.concatenate([slope_of * re, slope_of * im], axis=0))
+        back = dot_right(mix_back, mix_back[: 2 * rows], jnp.concatenate([slope_of * re, slope_of * im], axis=0))
         pieces = [
             (back[:rows, q * LANES : (q + 1) * LANES], back[rows:, q * LANES : (q + 1) * LANES])
             for q in range(outer)
@@ -214,9 +238,9 @@
             c, s = col_cos[k : k + 1], col_sin[k : k + 1]
             re = adjoint[k * rows : (k + 1) * rows, :LANES]
             im = adjoint[k * rows : (k + 1) * rows, LANES:]
-            term = jnp.concatenate([re * c - im * s, im * c + re * s], axis=1)
+            term = jnp.concatenate([im * c + re * s, re * c - im * s], axis=1)
             total[k] = term if total[k] is None else total[k] + term
-    parts = columns_inverse(jnp.concatenate(total, axis=0), inverse, mix_cos, mix_sin)
+    parts = columns_inverse(jnp.concatenate(total, axis=0), forward, mix_cos, mix_sin)
     grads = []
     for q in range(outer):
         (re, im), (wave_re, wave_im) = parts[q], waves[q]
@@ -230,8 +254,9 @@
 
 
 def fused_kernel(
-    sizes, slope_ref, fresnel_ref, volume_hbm, weight_ref, measured_hbm,
-    forward_ref, inverse_ref, small_ref, left_ref, right_ref, freq_ref, out_ref,
+    sizes, slope_ref, fresnel_ref, volume_hbm, weight_hbm, measured_hbm,
+    forward_hbm, small_hbm, left_hbm, right_hbm, freq_hbm, spread_ref, stack_ref,
+    weight_ref, forward_ref, small_ref, left_ref, right_ref, freq_ref, out_ref,
     volume_ref, own_ref, other_ref, fresnel_out, fresnel_in, send_ref, recv_ref, back_ref,
     local_sem, swap_send, swap_recv, send_sem, recv_sem, back_send, back_recv,
 ):
@@ -246,12 +271,24 @@
         there = lax.rem(me + step, devices)
         return there, (there // 2, lax.rem(there, 2))
 
+    weight_copy = pltpu.make_async_copy(
+        weight_hbm.at[:, pl.ds(pl.multiple_of(dist * rows_own, LANES), rows_own)],
+        weight_ref, local_sem.at[2],
+    )
+    weight_copy.start()
     volume_copy = pltpu.make_async_copy(volume_hbm, volume_ref, local_sem.at[0])
     volume_copy.start()
     own_copy = pltpu.make_async_copy(
         measured_hbm.at[pl.ds(dist * angles, angles)], own_ref, local_sem.at[1]
     )
     own_copy.start()
+    table_copies = []
+    for n, (source, target) in enumerate((
+        (forward_hbm, forward_ref), (small_hbm, small_ref), (left_hbm, left_ref),
+        (right_hbm, right_ref), (freq_hbm, freq_ref),
+    )):
+        table_copies.append(pltpu.make_async_copy(source, target, local_sem.at[3 + n]))
+        table_copies[n].start()
 
     def greet(step, carry):
         pl.semaphore_signal(
@@ -261,12 +298,17 @@
 
     lax.fori_loop(1, devices, greet, 0)
     fresnel_out[...] = jnp.full(fresnel_out.shape, fresnel_ref[0])
-    weights = weight_ref[:, pl.ds(pl.multiple_of(dist * rows_own, LANES), rows_own)]
+    weight_copy.wait()
+    weight_high, weight_low = halves(weight_ref[...])
+    weights = jnp.concatenate([weight_high, weight_low], axis=0)
+    stack_ref[...] = jnp.concatenate([weight_high, weight_low, weight_high], axis=0)
     volume_copy.wait()
-    for q in range(outer):
-        send_ref[pl.ds(q, angles_total, outer), :] = dot(
-            weights, volume_ref[:, q * LANES : (q + 1) * LANES]
-        )
+    for q in range(0, outer, 2):
+        high, low = halves(volume_ref[:, q * LANES : (q + 2) * LANES])
+        both = dot_narrow(weights, high) + dot_narrow(weights, low)
+        total = both[:angles_total] + both[angles_total:]
+        send_ref[pl.ds(q, angles_total, outer), :] = total[:, :LANES]
+        send_ref[pl.ds(q + 1, angles_total, outer), :] = total[:, LANES:]
     pl.semaphore_wait(barrier, devices - 1)
 
     def send(step, carry):
@@ -294,6 +336,8 @@
         ))
         swaps[n].start()
     own_copy.wait()
+    for copy in table_copies:
+        copy.wait()
     for swap in swaps:
         swap.wait()
     fresnels = [fresnel_out[0:1, 0:1], fresnel_in[0:1, 0:1]]
@@ -310,7 +354,7 @@
             for q in range(outer)
         ])
     tables = (
-        forward_ref[...], inverse_ref[...], (small_ref[0], small_ref[1], small_ref[2]),
+        (forward_ref[0], forward_ref[1]), (small_ref[0], small_ref[1], small_ref[2]),
         (left_ref[0], left_ref[1]), right_ref[...], freq_ref[...],
     )
     result = image_step(
@@ -339,6 +383,9 @@
     pltpu.make_async_copy(out_ref, out_ref, back_recv).wait()
     sent = out_ref.at[pl.ds(0, shift * piece)]
     pltpu.make_async_copy(sent, sent, back_send).wait()
+    for q in range(outer):
+        high, low = halves(out_ref[pl.ds(q, angles_total, outer), :])
+        spread_ref[:, q * LANES : (q + 1) * LANES] = jnp.concatenate([high, high, low], axis=0)
 
 
 def fused_call(slopes, fresnel, volume, weights, measured):
@@ -355,10 +402,16 @@
     dma = pltpu.SemaphoreType.DMA
     return pl.pallas_call(
         partial(fused_kernel, (angles, slices, outer, angles_total, rows_own, devices)),
-        out_shape=jax.ShapeDtypeStruct((devices * piece, LANES), f32),
-        in_specs=[smem, smem, hbm, vmem, hbm] + [vmem] * 6,
-        out_specs=vmem,
+        out_shape=(
+            jax.ShapeDtypeStruct((3 * angles_total, width), jnp.bfloat16),
+            jax.ShapeDtypeStruct((3 * angles_total, rows_own), jnp.bfloat16),
+        ),
+        in_specs=[smem, smem] + [hbm] * 8,
+        out_specs=(vmem, vmem),
         scratch_shapes=[
+            pltpu.VMEM((angles_total, rows_own), f32),
+            *[pltpu.VMEM(t.shape, t.dtype) for t in tables],
+            pltpu.VMEM((devices * piece, LANES), f32),
             pltpu.VMEM((rows_own, width), f32),
             pltpu.VMEM((angles, slices, width), f32),
             pltpu.VMEM((angles, slices, width), f32),
@@ -367,22 +420,17 @@
             pltpu.VMEM((devices * piece, LANES), f32),
             pltpu.VMEM((devices * piece, LANES), f32),
             pltpu.VMEM((slices * piece, LANES), f32),
-            dma((2,)), dma((2,)), dma((2,)), dma, dma, dma, dma,
+            dma((8,)), dma((2,)), dma((2,)), dma, dma, dma, dma,
         ],
         compiler_params=pltpu.CompilerParams(
-            vmem_limit_bytes=40 * 2**20, collective_id=0, has_side_effects=True
+            vmem_limit_bytes=58 * 2**20, collective_id=0, has_side_effects=True
         ),
     )(slopes, fresnel, volume, weights, measured, *[jnp.asarray(t) for t in tables])
 
 
 def shards(volume, row_weights, angle_slope, shear_index, shear_weight, fresnel, measured):
-    row_count, width = volume.shape[1], volume.shape[2]
-    own_weights = lax.dynamic_slice_in_dim(
-        row_weights, lax.axis_index("dist") * row_count, row_count, 1
-    )
-    spread = fused_call(angle_slope, fresnel, volume[0], row_weights, measured[0])
-    spread = spread.reshape(row_weights.shape[0], width)
-    return jnp.einsum("ay,ax->yx", own_weights, spread, precision=HIGHEST)[None]
+    spread, weights = fused_call(angle_slope, fresnel, volume[0], row_weights, measured[0])
+    return jnp.einsum("ky,kx->yx", weights, spread, preferred_element_type=jnp.float32)[None]
 
 
 def solution(mesh):

time: 40.8 us -> 30.6 us (0.75)
  local copies, waits for them, and re-layouts: 9.13 us -> 0 us
  Pallas kernels: 27.4 us -> 26.8 us
    unnamed x22 -> x0, local copies, waits for them, and re-layouts: 9.08 us -> none
    pallas_call x1, Pallas kernels: 27.4 us -> 26.8 us  [fused_call(): pl.pallas_call(partial(fused_kernel, (angles, slices, outer, angles_total...]
where the time goes in v3:
time: 30.6 us; the launch traced here: 30.4 us
  Pallas kernels  26.8 us (88%)
  matrix products  2.89 us (9%)
  between operations  0.66 us (2%)
    pallas_call x1, Pallas kernels, fused_call(): pl.pallas_call(partial(fused_kernel, (angles, slices, outer, angles_total...  26.8 us
    dot_general x1, matrix products, shards(): jnp.einsum('ky,kx->yx', weights, spread, preferred_element_type=jnp.float32)  2.89 us

profile of v3, /device:TPU:1, one launch (start us, length us, event | category | flops | bytes accessed | tf_op | source)
XLA Modules:
  0.0 30.4 jit_solution(6132723153875459478)
XLA Ops:
  0.7 26.8 %shard_map.100 = (bf16[192,1024]{1,0:T(8,128)(2,1)}, bf16[192,512]{1,0:T(8,128)(2,1)}) custom-call(s32[64]{0:T(128)} %slope_ref.1, f32[1]{0:T(128)S(6)} %copy.11.fresnel_ref, f32[512,1024]{1,0:T(8,128)} %bitcast.6, f32[64,1024]{1,0:T(8,128)} %weight_hbm.1, f32[4,16,1024]{2,1,0:T(8,128)} %bitcast.7, bf16[2,256,256]{2,1,0:T(8,128)(2,1)} %constant.10.clone.forward_hbm, ...), custom_call_target="tpu_custom_call" | custom-call | tf_op jit(solution)/shard_map/pallas_call | solution.py:403
  27.5 2.9 %convolution_bitcast_fusion = f32[1,512,1024]{2,1,0:T(8,128)} fusion(bf16[192,512]{1,0:T(8,128)(2,1)} %get-tuple-element.7, bf16[192,1024]{1,0:T(8,128)(2,1)} %get-tuple-element.8), kind=kOutput, calls=%fused_computation | convolution fusion | flops 201326592 | bytes 2686976 | tf_op jit(solution)/shard_map/ky,kx->yx/dot_general | solution.py:433

commit v4 on v3

--- a/solution.py
+++ b/solution.py
@@ -227,7 +227,7 @@
         stacked = jnp.concatenate([jnp.concatenate(part, axis=0) for part in parts], axis=1)
         field = dot_right(mix, mix[: 2 * rows], stacked * (1.0 / width))
         re, im = field[:rows], field[rows:]
-        slope_of = (re * re + im * im - measured[d]) * (4.0 / angles_total)
+        slope_of = (re * re + im * im - measured[d]()) * (4.0 / angles_total)
         back = dot_right(mix_back, mix_back[: 2 * rows], jnp.concatenate([slope_of * re, slope_of * im], axis=0))
         pieces = [
             (back[:rows, q * LANES : (q + 1) * LANES], back[rows:, q * LANES : (q + 1) * LANES])
@@ -255,27 +255,32 @@
 
 def fused_kernel(
     sizes, slope_ref, fresnel_ref, volume_hbm, weight_hbm, measured_hbm,
-    forward_hbm, small_hbm, left_hbm, right_hbm, freq_hbm, spread_ref, stack_ref,
-    weight_ref, forward_ref, small_ref, left_ref, right_ref, freq_ref, out_ref,
-    volume_ref, own_ref, other_ref, fresnel_out, fresnel_in, send_ref, recv_ref, back_ref,
-    local_sem, swap_send, swap_recv, send_sem, recv_sem, back_send, back_recv,
+    forward_hbm, small_hbm, left_hbm, right_hbm, freq_hbm, spread_ref, stack_hbm,
+    weight_ref, forward_ref, small_ref, left_ref, right_ref, freq_ref, out_ref, stack_ref,
+    volume_ref, own_ref, other_ref, fresnel_out, fresnel_in, keep_ref, give_ref, peer_ref,
+    recv_ref, back_ref,
+    local_sem, swap_send, swap_recv, peer_send, peer_recv, send_sem, recv_sem,
+    back_send, back_recv, pass_send, pass_recv, weight_sem,
 ):
-    angles, slices, outer, angles_total, rows_own, devices = sizes
+    angles, slices, outer, angles_total, rows_own, groups = sizes
     ang, dist = lax.axis_index("ang"), lax.axis_index("dist")
     me = ang * 2 + dist
     piece = angles * outer
     rows = angles * slices
+    half = groups // 2
+    chunk = half * piece
+    partner = (ang, 1 - dist)
+    mesh_ids = pl.DeviceIdType.MESH
     barrier = pltpu.get_barrier_semaphore()
 
-    def place_of(step):
-        there = lax.rem(me + step, devices)
-        return there, (there // 2, lax.rem(there, 2))
-
-    weight_copy = pltpu.make_async_copy(
-        weight_hbm.at[:, pl.ds(pl.multiple_of(dist * rows_own, LANES), rows_own)],
-        weight_ref, local_sem.at[2],
-    )
-    weight_copy.start()
+    weight_copies = []
+    for n in range(rows_own // LANES):
+        first_row = pl.multiple_of(dist * rows_own + n * LANES, LANES)
+        weight_copies.append(pltpu.make_async_copy(
+            weight_hbm.at[:, pl.ds(first_row, LANES)],
+            weight_ref.at[pl.ds(n * angles_total, angles_total)], weight_sem.at[n],
+        ))
+        weight_copies[n].start()
     volume_copy = pltpu.make_async_copy(volume_hbm, volume_ref, local_sem.at[0])
     volume_copy.start()
     own_copy = pltpu.make_async_copy(
@@ -289,42 +294,45 @@
     )):
         table_copies.append(pltpu.make_async_copy(source, target, local_sem.at[3 + n]))
         table_copies[n].start()
+    pl.semaphore_signal(barrier, inc=1, device_id=partner, device_id_type=mesh_ids)
 
     def greet(step, carry):
-        pl.semaphore_signal(
-            barrier, inc=1, device_id=place_of(step)[1], device_id_type=pl.DeviceIdType.MESH
-        )
+        there = lax.rem(ang + step, groups)
+        pl.semaphore_signal(barrier, inc=1, device_id=(there, dist), device_id_type=mesh_ids)
         return carry
 
-    lax.fori_loop(1, devices, greet, 0)
+    lax.fori_loop(1, groups, greet, 0)
     fresnel_out[...] = jnp.full(fresnel_out.shape, fresnel_ref[0])
-    weight_copy.wait()
-    weight_high, weight_low = halves(weight_ref[...])
+    for copy in weight_copies:
+        copy.wait()
+    columns = []
+    for n in range(rows_own // LANES):
+        blocks = []
+        for which in (dist, 1 - dist):
+            for a in range(angles):
+                for c in range(2):
+                    start = n * angles_total + c * 2 * angles + which * angles + a
+                    blocks.append(weight_ref[pl.ds(start, half, 4 * angles), :])
+        columns.append(jnp.concatenate(blocks, axis=0))
+    ordered = jnp.concatenate(columns, axis=1)
+    weight_high, weight_low = halves(ordered)
     weights = jnp.concatenate([weight_high, weight_low], axis=0)
-    stack_ref[...] = jnp.concatenate([weight_high, weight_low, weight_high], axis=0)
     volume_copy.wait()
     for q in range(0, outer, 2):
         high, low = halves(volume_ref[:, q * LANES : (q + 2) * LANES])
         both = dot_narrow(weights, high) + dot_narrow(weights, low)
         total = both[:angles_total] + both[angles_total:]
-        send_ref[pl.ds(q, angles_total, outer), :] = total[:, :LANES]
-        send_ref[pl.ds(q + 1, angles_total, outer), :] = total[:, LANES:]
-    pl.semaphore_wait(barrier, devices - 1)
-
-    def send(step, carry):
-        there, target = place_of(step)
-        pltpu.make_async_remote_copy(
-            src_ref=send_ref.at[pl.ds(there * piece, piece)],
-            dst_ref=recv_ref.at[pl.ds(me * piece, piece)],
-            send_sem=send_sem, recv_sem=recv_sem,
-            device_id=target, device_id_type=pl.DeviceIdType.MESH,
-        ).start()
-        return carry
-
-    lax.fori_loop(1, devices, send, 0)
-    pltpu.make_async_copy(
-        send_ref.at[pl.ds(me * piece, piece)], recv_ref.at[pl.ds(me * piece, piece)], recv_sem
-    ).start()
+        for rel, ref in enumerate((keep_ref, give_ref)):
+            for a in range(angles):
+                for c in range(2):
+                    first = ((rel * angles + a) * 2 + c) * half
+                    for p in range(2):
+                        place = c * chunk + a * outer + q + p
+                        ref[pl.ds(place, half, piece), :] = total[
+                            first : first + half, p * LANES : (p + 1) * LANES
+                        ]
+    pl.semaphore_wait(barrier, groups)
+
     swaps = []
     for n, (source, target) in enumerate((
         (fresnel_out, fresnel_in),
@@ -332,67 +340,144 @@
     )):
         swaps.append(pltpu.make_async_remote_copy(
             src_ref=source, dst_ref=target, send_sem=swap_send.at[n], recv_sem=swap_recv.at[n],
-            device_id=(ang, 1 - dist), device_id_type=pl.DeviceIdType.MESH,
+            device_id=partner, device_id_type=mesh_ids,
         ))
-        swaps[n].start()
+    peers = []
+    for c in range(2):
+        part = pl.ds(c * chunk, chunk)
+        peers.append(pltpu.make_async_remote_copy(
+            src_ref=give_ref.at[part], dst_ref=peer_ref.at[part],
+            send_sem=peer_send.at[c], recv_sem=peer_recv.at[c],
+            device_id=partner, device_id_type=mesh_ids,
+        ))
+        peers[c].start()
+    swaps[0].start()
+    swaps[1].start()
+
+    pad = stack_ref.shape[1] - 3 * angles_total
+    high_wide = weight_high.astype(jnp.float32)
+    tall = [high_wide, weight_low.astype(jnp.float32), high_wide]
+    if pad:
+        tall.append(jnp.zeros((pad, rows_own), jnp.float32))
+        spread_ref[3 * angles_total :, :] = jnp.zeros((pad, outer * LANES), jnp.bfloat16)
+    stack_ref[...] = jnp.concatenate(tall, axis=0).T.astype(jnp.bfloat16)
+    stack_copy = pltpu.make_async_copy(stack_ref, stack_hbm, local_sem.at[8])
+    stack_copy.start()
+
+    for c in range(2):
+        peers[c].wait()
+        part = pl.ds(c * chunk, chunk)
+        keep_ref[part, :] = keep_ref[part, :] + peer_ref[part, :]
+
+        def send(j):
+            there = lax.rem(ang // 2 + j, half)
+            return pltpu.make_async_remote_copy(
+                src_ref=keep_ref.at[pl.ds(c * chunk + there * piece, piece)],
+                dst_ref=recv_ref.at[pl.ds(ang * piece, piece)],
+                send_sem=send_sem, recv_sem=recv_sem,
+                device_id=(there * 2 + c, dist), device_id_type=mesh_ids,
+            )
+
+        def send_step(j, carry):
+            send(j).start()
+            return carry
+
+        lax.fori_loop(1, half, send_step, 0)
+
+        @pl.when(lax.rem(ang, 2) != c)
+        def _():
+            send(0).start()
+
+        @pl.when(lax.rem(ang, 2) == c)
+        def _():
+            pltpu.make_async_copy(
+                keep_ref.at[pl.ds(c * chunk + (ang // 2) * piece, piece)],
+                recv_ref.at[pl.ds(ang * piece, piece)], recv_sem,
+            ).start()
+
     own_copy.wait()
     for copy in table_copies:
         copy.wait()
-    for swap in swaps:
-        swap.wait()
+    swaps[0].wait()
     fresnels = [fresnel_out[0:1, 0:1], fresnel_in[0:1, 0:1]]
-    shift = devices - 1
     pltpu.make_async_copy(recv_ref, recv_ref, recv_sem).wait()
-    part = send_ref.at[pl.ds(0, shift * piece)]
-    pltpu.make_async_copy(part, part, send_sem).wait()
-    stride = 2 * piece
-    rays = []
-    for a in range(angles):
-        rays.append([
-            recv_ref[pl.ds(a * outer + q, slices, stride), :]
-            + recv_ref[pl.ds((angles + a) * outer + q, slices, stride), :]
-            for q in range(outer)
-        ])
+    rays = [
+        [recv_ref[pl.ds(a * outer + q, slices, piece), :] for q in range(outer)]
+        for a in range(angles)
+    ]
     tables = (
         (forward_ref[0], forward_ref[1]), (small_ref[0], small_ref[1], small_ref[2]),
         (left_ref[0], left_ref[1]), right_ref[...], freq_ref[...],
     )
+
+    def other_measured():
+        swaps[1].wait()
+        return other_ref[...].reshape(rows, outer * LANES)
+
     result = image_step(
         rays, [slope_ref[me * angles + a] for a in range(angles)], fresnels,
-        [own_ref[...].reshape(rows, outer * LANES), other_ref[...].reshape(rows, outer * LANES)],
+        [lambda: own_ref[...].reshape(rows, outer * LANES), other_measured],
         tables, angles_total,
     )
     for a in range(angles):
         for q in range(outer):
             back_ref[pl.ds(a * outer + q, slices, piece), :] = result[a][q]
 
+    parity = lax.rem(ang, 2)
+    mine = pl.ds(parity * chunk + (ang // 2) * piece, piece)
+
     def send_back(step, carry):
-        there, target = place_of(step)
+        there = lax.rem(ang + step, groups)
         pltpu.make_async_remote_copy(
-            src_ref=back_ref.at[pl.ds((there // 2) * piece, piece)],
-            dst_ref=out_ref.at[pl.ds(me * piece, piece)],
-            send_sem=back_send, recv_sem=back_recv,
-            device_id=target, device_id_type=pl.DeviceIdType.MESH,
+            src_ref=back_ref.at[pl.ds(there * piece, piece)], dst_ref=out_ref.at[mine],
+            send_sem=back_send, recv_sem=back_recv.at[parity],
+            device_id=(there, dist), device_id_type=mesh_ids,
         ).start()
         return carry
 
-    lax.fori_loop(1, devices, send_back, 0)
+    lax.fori_loop(1, groups, send_back, 0)
     pltpu.make_async_copy(
-        back_ref.at[pl.ds(ang * piece, piece)], out_ref.at[pl.ds(me * piece, piece)], back_recv
+        back_ref.at[pl.ds(ang * piece, piece)], out_ref.at[mine], back_recv.at[parity]
     ).start()
-    pltpu.make_async_copy(out_ref, out_ref, back_recv).wait()
-    sent = out_ref.at[pl.ds(0, shift * piece)]
-    pltpu.make_async_copy(sent, sent, back_send).wait()
-    for q in range(outer):
-        high, low = halves(out_ref[pl.ds(q, angles_total, outer), :])
-        spread_ref[:, q * LANES : (q + 1) * LANES] = jnp.concatenate([high, high, low], axis=0)
+    passes = []
+    for c in range(2):
+        part = out_ref.at[pl.ds(c * chunk, chunk)]
+        pltpu.make_async_copy(part, part, back_recv.at[c]).wait()
+        passes.append(pltpu.make_async_remote_copy(
+            src_ref=part, dst_ref=out_ref.at[pl.ds((2 + c) * chunk, chunk)],
+            send_sem=pass_send.at[c], recv_sem=pass_recv.at[c],
+            device_id=partner, device_id_type=mesh_ids,
+        ))
+        passes[c].start()
+
+    def stack_spread(rel):
+        for q in range(outer):
+            parts = [
+                out_ref[pl.ds(rel * 2 * chunk + a * outer + q, groups, piece), :]
+                for a in range(angles)
+            ]
+            high, low = halves(jnp.concatenate(parts, axis=0))
+            count = angles * groups
+            for n, value in enumerate((high, high, low)):
+                first = n * angles_total + rel * count
+                spread_ref[first : first + count, q * LANES : (q + 1) * LANES] = value
+
+    stack_spread(0)
+    for copy in passes:
+        copy.wait()
+    stack_spread(1)
+    for ref, sem in ((keep_ref, send_sem), (back_ref, back_send)):
+        sent = ref.at[pl.ds(0, (groups - 1) * piece)]
+        pltpu.make_async_copy(sent, sent, sem).wait()
+    stack_copy.wait()
 
 
 def fused_call(slopes, fresnel, volume, weights, measured):
     group, slices, width = measured.shape
     angles, outer = group // 2, width // LANES
     angles_total, rows_own = weights.shape[0], volume.shape[0]
-    devices = angles_total // angles
+    groups = angles_total // group
+    depth = -(-3 * angles_total // 256) * 256
     piece = angles * outer
     tables = column_tables(width) + row_tables(slices, angles)
     smem = pl.BlockSpec(memory_space=pltpu.SMEM)
@@ -401,26 +486,27 @@
     f32 = jnp.float32
     dma = pltpu.SemaphoreType.DMA
     return pl.pallas_call(
-        partial(fused_kernel, (angles, slices, outer, angles_total, rows_own, devices)),
+        partial(fused_kernel, (angles, slices, outer, angles_total, rows_own, groups)),
         out_shape=(
-            jax.ShapeDtypeStruct((3 * angles_total, width), jnp.bfloat16),
-            jax.ShapeDtypeStruct((3 * angles_total, rows_own), jnp.bfloat16),
+            jax.ShapeDtypeStruct((depth, width), jnp.bfloat16),
+            jax.ShapeDtypeStruct((rows_own, depth), jnp.bfloat16),
         ),
         in_specs=[smem, smem] + [hbm] * 8,
-        out_specs=(vmem, vmem),
+        out_specs=(vmem, hbm),
         scratch_shapes=[
-            pltpu.VMEM((angles_total, rows_own), f32),
+            pltpu.VMEM((rows_own // LANES * angles_total, LANES), f32),
             *[pltpu.VMEM(t.shape, t.dtype) for t in tables],
-            pltpu.VMEM((devices * piece, LANES), f32),
+            pltpu.VMEM((2 * groups * piece, LANES), f32),
+            pltpu.VMEM((rows_own, depth), jnp.bfloat16),
             pltpu.VMEM((rows_own, width), f32),
             pltpu.VMEM((angles, slices, width), f32),
             pltpu.VMEM((angles, slices, width), f32),
             pltpu.VMEM((8, LANES), f32),
             pltpu.VMEM((8, LANES), f32),
-            pltpu.VMEM((devices * piece, LANES), f32),
-            pltpu.VMEM((devices * piece, LANES), f32),
-            pltpu.VMEM((slices * piece, LANES), f32),
-            dma((8,)), dma((2,)), dma((2,)), dma, dma, dma, dma,
+            *[pltpu.VMEM((groups * piece, LANES), f32) for _ in range(3)],
+            *[pltpu.VMEM((slices * piece, LANES), f32) for _ in range(2)],
+            dma((9,)), *[dma((2,)) for _ in range(4)], dma, dma,
+            dma, *[dma((2,)) for _ in range(3)], dma((rows_own // LANES,)),
         ],
         compiler_params=pltpu.CompilerParams(
             vmem_limit_bytes=58 * 2**20, collective_id=0, has_side_effects=True
@@ -430,7 +516,7 @@
 
 def shards(volume, row_weights, angle_slope, shear_index, shear_weight, fresnel, measured):
     spread, weights = fused_call(angle_slope, fresnel, volume[0], row_weights, measured[0])
-    return jnp.einsum("ky,kx->yx", weights, spread, preferred_element_type=jnp.float32)[None]
+    return jnp.einsum("yk,kx->yx", weights, spread, preferred_element_type=jnp.float32)[None]
 
 
 def solution(mesh):

time: 30.6 us -> 33.8 us (1.10)
  the two profiles are of different devices: /device:TPU:1 before, /device:TPU:0 now
where the time goes in v4:
time: 33.8 us; the launch traced here: 33.6 us
  Pallas kernels  30.1 us (89%)
  matrix products  2.88 us (9%)
  between operations  0.66 us (2%)
    pallas_call x1, Pallas kernels, fused_call(): pl.pallas_call(partial(fused_kernel, (angles, slices, outer, angles_total...  30.1 us
    dot_general x1, matrix products, shards(): jnp.einsum('yk,kx->yx', weights, spread, preferred_element_type=jnp.float32)  2.88 us

profile of v4, /device:TPU:0, one launch (start us, length us, event | category | flops | bytes accessed | tf_op | source)
XLA Modules:
  0.0 33.6 jit_solution(4536890906876144087)
XLA Ops:
  0.7 30.1 %shard_map.100 = (bf16[256,1024]{1,0:T(8,128)(2,1)}, bf16[512,256]{1,0:T(8,128)(2,1)}) custom-call(s32[64]{0:T(128)} %slope_ref.1, f32[1]{0:T(128)S(6)} %copy.11.fresnel_ref, f32[512,1024]{1,0:T(8,128)} %bitcast.6, f32[64,1024]{1,0:T(8,128)} %weight_hbm.1, f32[4,16,1024]{2,1,0:T(8,128)} %bitcast.7, bf16[2,256,256]{2,1,0:T(8,128)(2,1)} %constant.10.clone.forward_hbm, ...), custom_call_target="tpu_custom_call" | custom-call | tf_op jit(solution)/shard_map/pallas_call | solution.py:488
  30.7 2.9 %convolution_bitcast_fusion = f32[1,512,1024]{2,1,0:T(8,128)} fusion(bf16[512,256]{1,0:T(8,128)(2,1)} %get-tuple-element.7, bf16[256,1024]{1,0:T(8,128)(2,1)} %get-tuple-element.8), kind=kOutput, calls=%fused_computation | convolution fusion | flops 268435456 | bytes 2883584 | tf_op jit(solution)/shard_map/yk,kx->yx/dot_general | solution.py:519

commit v5 on v3

--- a/solution.py
+++ b/solution.py
@@ -227,7 +227,7 @@
         stacked = jnp.concatenate([jnp.concatenate(part, axis=0) for part in parts], axis=1)
         field = dot_right(mix, mix[: 2 * rows], stacked * (1.0 / width))
         re, im = field[:rows], field[rows:]
-        slope_of = (re * re + im * im - measured[d]) * (4.0 / angles_total)
+        slope_of = (re * re + im * im - measured[d]()) * (4.0 / angles_total)
         back = dot_right(mix_back, mix_back[: 2 * rows], jnp.concatenate([slope_of * re, slope_of * im], axis=0))
         pieces = [
             (back[:rows, q * LANES : (q + 1) * LANES], back[rows:, q * LANES : (q + 1) * LANES])
@@ -321,10 +321,6 @@
         ).start()
         return carry
 
-    lax.fori_loop(1, devices, send, 0)
-    pltpu.make_async_copy(
-        send_ref.at[pl.ds(me * piece, piece)], recv_ref.at[pl.ds(me * piece, piece)], recv_sem
-    ).start()
     swaps = []
     for n, (source, target) in enumerate((
         (fresnel_out, fresnel_in),
@@ -334,12 +330,16 @@
             src_ref=source, dst_ref=target, send_sem=swap_send.at[n], recv_sem=swap_recv.at[n],
             device_id=(ang, 1 - dist), device_id_type=pl.DeviceIdType.MESH,
         ))
-        swaps[n].start()
+    swaps[0].start()
+    lax.fori_loop(1, devices, send, 0)
+    pltpu.make_async_copy(
+        send_ref.at[pl.ds(me * piece, piece)], recv_ref.at[pl.ds(me * piece, piece)], recv_sem
+    ).start()
+    swaps[1].start()
     own_copy.wait()
     for copy in table_copies:
         copy.wait()
-    for swap in swaps:
-        swap.wait()
+    swaps[0].wait()
     fresnels = [fresnel_out[0:1, 0:1], fresnel_in[0:1, 0:1]]
     shift = devices - 1
     pltpu.make_async_copy(recv_ref, recv_ref, recv_sem).wait()
@@ -357,9 +357,13 @@
         (forward_ref[0], forward_ref[1]), (small_ref[0], small_ref[1], small_ref[2]),
         (left_ref[0], left_ref[1]), right_ref[...], freq_ref[...],
     )
+    def other_measured():
+        swaps[1].wait()
+        return other_ref[...].reshape(rows, outer * LANES)
+
     result = image_step(
         rays, [slope_ref[me * angles + a] for a in range(angles)], fresnels,
-        [own_ref[...].reshape(rows, outer * LANES), other_ref[...].reshape(rows, outer * LANES)],
+        [lambda: own_ref[...].reshape(rows, outer * LANES), other_measured],
         tables, angles_total,
     )
     for a in range(angles):

time: 30.6 us -> 30.2 us (0.987); the launches traced: 30.4 us -> 29.6 us
  Pallas kernels: 26.8 us -> 26.1 us
    pallas_call x1, Pallas kernels: 26.8 us -> 26.1 us  [fused_call(): pl.pallas_call(partial(fused_kernel, (angles, slices, outer, angles_total...]
where the time goes in v5:
time: 30.2 us; the launch traced here: 29.6 us
  Pallas kernels  26.1 us (86%)
  matrix products  2.89 us (10%)
  between operations  0.66 us (2%)
    pallas_call x1, Pallas kernels, fused_call(): pl.pallas_call(partial(fused_kernel, (angles, slices, outer, angles_total...  26.1 us
    dot_general x1, matrix products, shards(): jnp.einsum('ky,kx->yx', weights, spread, preferred_element_type=jnp.float32)  2.89 us

profile of v5, /device:TPU:1, one launch (start us, length us, event | category | flops | bytes accessed | tf_op | source)
XLA Modules:
  0.0 29.6 jit_solution(12310179886575387681)
XLA Ops:
  0.7 26.1 %shard_map.100 = (bf16[192,1024]{1,0:T(8,128)(2,1)}, bf16[192,512]{1,0:T(8,128)(2,1)}) custom-call(s32[64]{0:T(128)} %slope_ref.1, f32[1]{0:T(128)S(6)} %copy.11.fresnel_ref, f32[512,1024]{1,0:T(8,128)} %bitcast.6, f32[64,1024]{1,0:T(8,128)} %weight_hbm.1, f32[4,16,1024]{2,1,0:T(8,128)} %bitcast.7, bf16[2,256,256]{2,1,0:T(8,128)(2,1)} %constant.10.clone.forward_hbm, ...), custom_call_target="tpu_custom_call" | custom-call | tf_op jit(solution)/shard_map/pallas_call | solution.py:407
  26.7 2.9 %convolution_bitcast_fusion = f32[1,512,1024]{2,1,0:T(8,128)} fusion(bf16[192,512]{1,0:T(8,128)(2,1)} %get-tuple-element.7, bf16[192,1024]{1,0:T(8,128)(2,1)} %get-tuple-element.8), kind=kOutput, calls=%fused_computation | convolution fusion | flops 201326592 | bytes 2686976 | tf_op jit(solution)/shard_map/ky,kx->yx/dot_general | solution.py:437
